TPU v7x, 1024 devices: a whole 4x8x16 slice. The times are simulated.
1024 devices in a mesh: lgroup: 8 (over z_hi, core), row: 128 (over x, y, z_lo).
Axes of the slice: x: 4, y: 8, z: 16 (z_hi: 4, z_lo: 4; z = z_hi * 4 + z_lo), core: 2. Of those that a mesh axis runs over, the one named last changes fastest.
Arguments:
- psi_in: float32 [2, 512, 1024, 128], P(None, 'lgroup', 'row'), may hold values from -6 to 6
- channels: int32 [8, 2, 64], P('lgroup'), may hold values from -1 to 11, as said below
- multipole: float32 [8, 3, 64, 64], P('lgroup'), may hold values from -0.18 to 0.18
- dipole: float32 [8, 2, 64, 64], P('lgroup'), may hold values from -0.36 to 0.36
Outputs:
- psi_out: float32 [2, 512, 1024, 128], P(None, 'lgroup', 'row')
Inputs may be any that keep to these rules, and one draw needn't show every extreme that they name: In each block the live channels fill the first slots and hold l1 and l2 of 0 to 11; the other slots hold -1 in both entries. Each block has 64 / 4 (rounded down) or more live slots, and some block has all 64 live.
All inputs are finite; a program needn't handle non-finite values.
Results may differ from a plain program's by a relative error of at most 0.0001.
Values sent between devices are 32-bit elements; how exact they have to be, the bound alone decides.
No kernel may reach another device: no remote copies, remote signals or barrier semaphores. Data moves between devices by JAX's collectives and lax.ppermute only.
A program may use at most 32 MiB of HBM per device.

v0:
```python
import jax
import jax.numpy as jnp
from jax import lax
from jax.sharding import PartitionSpec as P

ORDER = 4


kinetic_scale = 0.2
coulomb_charge = 4.0
radius_offset = 16.0
center_weight = -2.5
near_weight = 4.0 / 3.0
far_weight = -1.0 / 12.0


def extended(block, sides, width):
    for axis, dim in sides:
        count = lax.axis_size(axis)
        forward = [(i, i + 1) for i in range(count - 1)]
        backward = [(target, source) for source, target in forward]
        low = lax.ppermute(
            lax.slice_in_dim(block, block.shape[dim] - width, None, axis=dim), axis, forward
        )
        high = lax.ppermute(lax.slice_in_dim(block, 0, width, axis=dim), axis, backward)
        block = jnp.concatenate([low, block, high], axis=dim)
    return block


def passed_along(value, axis, by):
    count = lax.axis_size(axis)
    pairs = [(i, i + by) for i in range(count) if 0 <= i + by < count]
    return lax.ppermute(value, axis, pairs)


def local(psi_in, channels, multipole, dipole):
    rows_one = psi_in.shape[2]
    rows_two = psi_in.shape[3]
    total_rows = lax.axis_size("row") * rows_one
    first_row = lax.axis_index("row") * rows_one
    live_mask = (channels[0, 0, :] >= 0).astype(jnp.float32)[None, :, None, None]
    ang_one = channels[0, 0, :].astype(jnp.float32)
    ang_two = channels[0, 1, :].astype(jnp.float32)
    radius_one = (first_row + jnp.arange(rows_one)).astype(jnp.float32) + radius_offset
    radius_two = jnp.arange(rows_two).astype(jnp.float32) + radius_offset
    potential = (
        (ang_one * (ang_one + 1.0))[:, None, None] / (radius_one**2)[:, None]
        + (ang_two * (ang_two + 1.0))[:, None, None] / (radius_two**2)[None, :]
        - coulomb_charge * (1.0 / radius_one[:, None] + 1.0 / radius_two[None, :])
    )
    radius_ratio = jnp.minimum(radius_one[:, None], radius_two[None, :]) / jnp.maximum(
        radius_one[:, None], radius_two[None, :]
    )
    coupling = 0.5 * (multipole[0] + jnp.swapaxes(multipole[0], -1, -2))
    weight_one = (radius_one / (total_rows + radius_offset))[:, None]
    weight_two = (radius_two / (rows_two + radius_offset))[None, :]
    mat_a = dipole[0, 0]
    mat_b = dipole[0, 1]
    highest = lax.Precision.HIGHEST
    start = psi_in * live_mask
    total = start
    term = start
    for order_index in range(1, ORDER + 1):
        rimmed = extended(term, (("row", 2),), 2)
        padded = jnp.pad(rimmed, ((0, 0), (0, 0), (0, 0), (2, 2)))
        laplace = 2.0 * center_weight * term
        laplace = laplace + near_weight * (
            padded[..., 3:-1, 2:-2]
            + padded[..., 1:-3, 2:-2]
            + padded[..., 2:-2, 3:-1]
            + padded[..., 2:-2, 1:-3]
        )
        laplace = laplace + far_weight * (
            padded[..., 4:, 2:-2]
            + padded[..., :-4, 2:-2]
            + padded[..., 2:-2, 4:]
            + padded[..., 2:-2, :-4]
        )
        result = -kinetic_scale * laplace + potential * term
        for degree in range(coupling.shape[0]):
            result = result + radius_ratio**degree * jnp.einsum(
                "cd,sdij->scij", coupling[degree], term, precision=highest
            )
        from_above = passed_along(term, "lgroup", -1)
        result = result + weight_one * jnp.einsum(
            "cd,sdij->scij", mat_a, from_above, precision=highest
        )
        result = result + weight_two * jnp.einsum(
            "cd,sdij->scij", mat_b, from_above, precision=highest
        )
        outgoing = weight_one * jnp.einsum(
            "dc,sdij->scij", mat_a, term, precision=highest
        ) + weight_two * jnp.einsum("dc,sdij->scij", mat_b, term, precision=highest)
        from_below = passed_along(outgoing, "lgroup", 1)
        result = result + from_below
        image = result * live_mask
        term = jnp.stack([image[1], -image[0]]) / float(order_index)
        total = total + term
    return total


def solution(mesh):
    placed = (
        P(None, "lgroup", "row", None),
        P("lgroup", None, None),
        P("lgroup", None, None, None),
        P("lgroup", None, None, None),
    )
    return jax.shard_map(
        local, mesh=mesh, in_specs=placed, out_specs=P(None, "lgroup", "row", None), check_vma=False
    )
```

profile of v0, /device:TPU:353, one launch (start us, length us, event | category | flops | bytes accessed | tf_op | source)
XLA Modules:
  0.0 173.1 jit_solution(10872817119539836038)
XLA Ops:
  0.0 0.7 fusion.136
  0.7 1.2 copy_multiply_fusion
  2.0 2.7 %collective-permute-start.2 = (f32[2,64,8,128]{3,1,2,0:T(8,128)S(1)}, f32[2,64,8,128]{3,1,2,0:T(8,128)S(1)}, u32[]{:S(2)}, u32[]{:S(2)}) collective-permute-start(f32[2,64,8,128]{3,1,2,0:T(8,128)S(1)} %copy_multiply_fusion), channel_id=1, source_target_pairs={{128,0},{256,128},{384,256},{512,384},{640,512},{768,640},{896,768... | collective-permute-start | bytes 1572872 | tf_op jit(solution)/shard_map/ppermute | solution.py:33
  4.7 1.9 %collective-permute-start = (f32[2,64,2,128]{3,1,2,0:T(8,128)S(1)}, f32[2,64,2,128]{3,1,2,0:T(8,128)S(1)}, u32[]{:S(2)}, u32[]{:S(2)}) collective-permute-start(f32[2,64,2,128]{3,1,2,0:T(8,128)S(1)} %get-tuple-element.21), channel_id=1, source_target_pairs={{1,0},{2,1},{3,2},{4,3},{5,4},{6,5},{7,6},{8,7},{9,8},{10,9},{11,1... | collective-permute-start | bytes 393224 | tf_op jit(solution)/shard_map/ppermute | solution.py:25
  6.6 4.0 %collective-permute-start.1 = (f32[2,64,2,128]{3,1,2,0:T(8,128)S(1)}, f32[2,64,2,128]{3,1,2,0:T(8,128)S(1)}, u32[]{:S(2)}, u32[]{:S(2)}) collective-permute-start(f32[2,64,2,128]{3,1,2,0:T(8,128)S(1)} %get-tuple-element.22), channel_id=1, source_target_pairs={{0,1},{1,2},{2,3},{3,4},{4,5},{5,6},{6,7},{7,8},{8,9},{9,10},{10,1... | collective-permute-start | bytes 393224 | tf_op jit(solution)/shard_map/ppermute | solution.py:22
  12.0 9.6 %collective-permute-start.3 = (f32[2,64,8,128]{3,1,2,0:T(8,128)S(1)}, f32[2,64,8,128]{3,1,2,0:T(8,128)S(1)}, u32[]{:S(2)}, u32[]{:S(2)}) collective-permute-start(f32[2,64,8,128]{3,1,2,0:T(8,128)S(1)} %fusion.44), channel_id=1, source_target_pairs={{0,128},{128,256},{256,384},{384,512},{512,640},{640,768},{768,896... | collective-permute-start | bytes 1572872 | tf_op jit(solution)/shard_map/ppermute | solution.py:33
  24.0 0.9 fusion.3
  24.9 12.7 %collective-permute-done.2 = f32[2,64,8,128]{3,1,2,0:T(8,128)S(1)} collective-permute-done((f32[2,64,8,128]{3,1,2,0:T(8,128)S(1)}, f32[2,64,8,128]{3,1,2,0:T(8,128)S(1)}, u32[]{:S(2)}, u32[]{:S(2)}) %collective-permute-start.2) | collective-permute-done | bytes 524320 | tf_op jit(solution)/shard_map/ppermute | solution.py:33
  38.3 6.3 %collective-permute-done.3 = f32[2,64,8,128]{3,1,2,0:T(8,128)S(1)} collective-permute-done((f32[2,64,8,128]{3,1,2,0:T(8,128)S(1)}, f32[2,64,8,128]{3,1,2,0:T(8,128)S(1)}, u32[]{:S(2)}, u32[]{:S(2)}) %collective-permute-start.3) | collective-permute-done | bytes 524320 | tf_op jit(solution)/shard_map/ppermute | solution.py:33
  46.6 1.9 %collective-permute-start.6 = (f32[2,64,8,128]{3,1,2,0:T(8,128)S(1)}, f32[2,64,8,128]{3,1,2,0:T(8,128)S(1)}, u32[]{:S(2)}, u32[]{:S(2)}) collective-permute-start(f32[2,64,8,128]{3,1,2,0:T(8,128)S(1)} %pad_maximum_fusion), channel_id=1, source_target_pairs={{128,0},{256,128},{384,256},{512,384},{640,512},{768,640},{896,768... | collective-permute-start | bytes 1572872 | tf_op jit(solution)/shard_map/ppermute | solution.py:33
  48.5 1.9 %collective-permute-start.4 = (f32[2,64,2,128]{3,1,2,0:T(8,128)S(1)}, f32[2,64,2,128]{3,1,2,0:T(8,128)S(1)}, u32[]{:S(2)}, u32[]{:S(2)}) collective-permute-start(f32[2,64,2,128]{3,1,2,0:T(8,128)S(1)} %get-tuple-element.18), channel_id=1, source_target_pairs={{1,0},{2,1},{3,2},{4,3},{5,4},{6,5},{7,6},{8,7},{9,8},{10,9},{11,1... | collective-permute-start | bytes 393224 | tf_op jit(solution)/shard_map/ppermute | solution.py:25
  50.4 3.4 %collective-permute-start.5 = (f32[2,64,2,128]{3,1,2,0:T(8,128)S(1)}, f32[2,64,2,128]{3,1,2,0:T(8,128)S(1)}, u32[]{:S(2)}, u32[]{:S(2)}) collective-permute-start(f32[2,64,2,128]{3,1,2,0:T(8,128)S(1)} %get-tuple-element.17), channel_id=1, source_target_pairs={{0,1},{1,2},{2,3},{3,4},{4,5},{5,6},{6,7},{7,8},{8,9},{9,10},{10,1... | collective-permute-start | bytes 393224 | tf_op jit(solution)/shard_map/ppermute | solution.py:22
  54.4 9.1 %collective-permute-start.7 = (f32[2,64,8,128]{3,1,2,0:T(8,128)S(1)}, f32[2,64,8,128]{3,1,2,0:T(8,128)S(1)}, u32[]{:S(2)}, u32[]{:S(2)}) collective-permute-start(f32[2,64,8,128]{3,1,2,0:T(8,128)S(1)} %fusion.34), channel_id=1, source_target_pairs={{0,128},{128,256},{256,384},{384,512},{512,640},{640,768},{768,896... | collective-permute-start | bytes 1572872 | tf_op jit(solution)/shard_map/ppermute | solution.py:33
  65.0 1.0 fusion.6
  66.0 13.8 %collective-permute-done.6 = f32[2,64,8,128]{3,1,2,0:T(8,128)S(1)} collective-permute-done((f32[2,64,8,128]{3,1,2,0:T(8,128)S(1)}, f32[2,64,8,128]{3,1,2,0:T(8,128)S(1)}, u32[]{:S(2)}, u32[]{:S(2)}) %collective-permute-start.6) | collective-permute-done | bytes 524320 | tf_op jit(solution)/shard_map/ppermute | solution.py:33
  80.4 6.0 %collective-permute-done.7 = f32[2,64,8,128]{3,1,2,0:T(8,128)S(1)} collective-permute-done((f32[2,64,8,128]{3,1,2,0:T(8,128)S(1)}, f32[2,64,8,128]{3,1,2,0:T(8,128)S(1)}, u32[]{:S(2)}, u32[]{:S(2)}) %collective-permute-start.7) | collective-permute-done | bytes 524320 | tf_op jit(solution)/shard_map/ppermute | solution.py:33
  87.8 1.9 %collective-permute-start.10 = (f32[2,64,8,128]{3,1,2,0:T(8,128)S(1)}, f32[2,64,8,128]{3,1,2,0:T(8,128)S(1)}, u32[]{:S(2)}, u32[]{:S(2)}) collective-permute-start(f32[2,64,8,128]{3,1,2,0:T(8,128)S(1)} %fusion.97), channel_id=1, source_target_pairs={{128,0},{256,128},{384,256},{512,384},{640,512},{768,640},{896,768... | collective-permute-start | bytes 1572872 | tf_op jit(solution)/shard_map/ppermute | solution.py:33
  90.4 1.9 %collective-permute-start.8 = (f32[2,64,2,128]{3,1,2,0:T(8,128)S(1)}, f32[2,64,2,128]{3,1,2,0:T(8,128)S(1)}, u32[]{:S(2)}, u32[]{:S(2)}) collective-permute-start(f32[2,64,2,128]{3,1,2,0:T(8,128)S(1)} %get-tuple-element.11), channel_id=1, source_target_pairs={{1,0},{2,1},{3,2},{4,3},{5,4},{6,5},{7,6},{8,7},{9,8},{10,9},{11,1... | collective-permute-start | bytes 393224 | tf_op jit(solution)/shard_map/ppermute | solution.py:25
  92.3 3.4 %collective-permute-start.9 = (f32[2,64,2,128]{3,1,2,0:T(8,128)S(1)}, f32[2,64,2,128]{3,1,2,0:T(8,128)S(1)}, u32[]{:S(2)}, u32[]{:S(2)}) collective-permute-start(f32[2,64,2,128]{3,1,2,0:T(8,128)S(1)} %get-tuple-element.12), channel_id=1, source_target_pairs={{0,1},{1,2},{2,3},{3,4},{4,5},{5,6},{6,7},{7,8},{8,9},{9,10},{10,1... | collective-permute-start | bytes 393224 | tf_op jit(solution)/shard_map/ppermute | solution.py:22
  97.0 9.0 %collective-permute-start.11 = (f32[2,64,8,128]{3,1,2,0:T(8,128)S(1)}, f32[2,64,8,128]{3,1,2,0:T(8,128)S(1)}, u32[]{:S(2)}, u32[]{:S(2)}) collective-permute-start(f32[2,64,8,128]{3,1,2,0:T(8,128)S(1)} %fusion.24), channel_id=1, source_target_pairs={{0,128},{128,256},{256,384},{384,512},{512,640},{640,768},{768,896... | collective-permute-start | bytes 1572872 | tf_op jit(solution)/shard_map/ppermute | solution.py:33
  106.4 0.9 fusion.9
  107.4 7.3 %collective-permute-done.10 = f32[2,64,8,128]{3,1,2,0:T(8,128)S(1)} collective-permute-done((f32[2,64,8,128]{3,1,2,0:T(8,128)S(1)}, f32[2,64,8,128]{3,1,2,0:T(8,128)S(1)}, u32[]{:S(2)}, u32[]{:S(2)}) %collective-permute-start.10) | collective-permute-done | bytes 524320 | tf_op jit(solution)/shard_map/ppermute | solution.py:33
  115.3 13.5 %collective-permute-done.11 = f32[2,64,8,128]{3,1,2,0:T(8,128)S(1)} collective-permute-done((f32[2,64,8,128]{3,1,2,0:T(8,128)S(1)}, f32[2,64,8,128]{3,1,2,0:T(8,128)S(1)}, u32[]{:S(2)}, u32[]{:S(2)}) %collective-permute-start.11) | collective-permute-done | bytes 524320 | tf_op jit(solution)/shard_map/ppermute | solution.py:33
  130.2 1.9 %collective-permute-start.14 = (f32[2,64,8,128]{3,1,2,0:T(8,128)S(1)}, f32[2,64,8,128]{3,1,2,0:T(8,128)S(1)}, u32[]{:S(2)}, u32[]{:S(2)}) collective-permute-start(f32[2,64,8,128]{3,1,2,0:T(8,128)S(1)} %fusion.96), channel_id=1, source_target_pairs={{128,0},{256,128},{384,256},{512,384},{640,512},{768,640},{896,768... | collective-permute-start | bytes 1572872 | tf_op jit(solution)/shard_map/ppermute | solution.py:33
  132.7 1.9 %collective-permute-start.12 = (f32[2,64,2,128]{3,1,2,0:T(8,128)S(1)}, f32[2,64,2,128]{3,1,2,0:T(8,128)S(1)}, u32[]{:S(2)}, u32[]{:S(2)}) collective-permute-start(f32[2,64,2,128]{3,1,2,0:T(8,128)S(1)} %get-tuple-element.7), channel_id=1, source_target_pairs={{1,0},{2,1},{3,2},{4,3},{5,4},{6,5},{7,6},{8,7},{9,8},{10,9},{11,1... | collective-permute-start | bytes 393224 | tf_op jit(solution)/shard_map/ppermute | solution.py:25
  134.7 3.4 %collective-permute-start.13 = (f32[2,64,2,128]{3,1,2,0:T(8,128)S(1)}, f32[2,64,2,128]{3,1,2,0:T(8,128)S(1)}, u32[]{:S(2)}, u32[]{:S(2)}) collective-permute-start(f32[2,64,2,128]{3,1,2,0:T(8,128)S(1)} %get-tuple-element.8), channel_id=1, source_target_pairs={{0,1},{1,2},{2,3},{3,4},{4,5},{5,6},{6,7},{7,8},{8,9},{9,10},{10,1... | collective-permute-start | bytes 393224 | tf_op jit(solution)/shard_map/ppermute | solution.py:22
  139.3 9.1 %collective-permute-start.15 = (f32[2,64,8,128]{3,1,2,0:T(8,128)S(1)}, f32[2,64,8,128]{3,1,2,0:T(8,128)S(1)}, u32[]{:S(2)}, u32[]{:S(2)}) collective-permute-start(f32[2,64,8,128]{3,1,2,0:T(8,128)S(1)} %fusion.14), channel_id=1, source_target_pairs={{0,128},{128,256},{256,384},{384,512},{512,640},{640,768},{768,896... | collective-permute-start | bytes 1572872 | tf_op jit(solution)/shard_map/ppermute | solution.py:33
  148.4 6.1 %collective-permute-done.12 = f32[2,64,2,128]{3,1,2,0:T(8,128)S(1)} collective-permute-done((f32[2,64,2,128]{3,1,2,0:T(8,128)S(1)}, f32[2,64,2,128]{3,1,2,0:T(8,128)S(1)}, u32[]{:S(2)}, u32[]{:S(2)}) %collective-permute-start.12) | collective-permute-done | bytes 131104 | tf_op jit(solution)/shard_map/ppermute | solution.py:25
  154.9 0.9 fusion.12
  156.5 14.4 %collective-permute-done.15 = f32[2,64,8,128]{3,1,2,0:T(8,128)S(1)} collective-permute-done((f32[2,64,8,128]{3,1,2,0:T(8,128)S(1)}, f32[2,64,8,128]{3,1,2,0:T(8,128)S(1)}, u32[]{:S(2)}, u32[]{:S(2)}) %collective-permute-start.15) | collective-permute-done | bytes 524320 | tf_op jit(solution)/shard_map/ppermute | solution.py:33
  170.9 0.7 fusion.18
  172.0 1.1 copy.16
  (71 shorter events, 18.0 us)
Async XLA Ops:
  0.0 10.7 %copy-start = (f32[1,2,64,64]{3,2,1,0:T(8,128)S(1)}, f32[1,2,64,64]{3,2,1,0:T(8,128)}, u32[]{:S(2)}) copy-start(f32[1,2,64,64]{3,2,1,0:T(8,128)} %param.7) | copy-start | bytes 98308
  1.9 19.6 %copy-start.3 = (s32[1,2,64]{2,1,0:T(2,128)S(1)}, s32[1,2,64]{2,1,0:T(2,128)}, u32[]{:S(2)}) copy-start(s32[1,2,64]{2,1,0:T(2,128)} %param.5) | copy-start | bytes 1540
  1.9 19.7 %copy-start.2 = (f32[1,3,64,64]{3,2,1,0:T(8,128)S(1)}, f32[1,3,64,64]{3,2,1,0:T(8,128)}, u32[]{:S(2)}) copy-start(f32[1,3,64,64]{3,2,1,0:T(8,128)} %param.6) | copy-start | bytes 147460
  2.0 35.7 %collective-permute-start.2 = (f32[2,64,8,128]{3,1,2,0:T(8,128)S(1)}, f32[2,64,8,128]{3,1,2,0:T(8,128)S(1)}, u32[]{:S(2)}, u32[]{:S(2)}) collective-permute-start(f32[2,64,8,128]{3,1,2,0:T(8,128)S(1)} %copy_multiply_fusion), channel_id=1, source_target_pairs={{128,0},{256,128},{384,256},{512,384},{640,512},{768,640},{896,768... | collective-permute-start | bytes 1572872 | tf_op jit(solution)/shard_map/ppermute | solution.py:33
  4.7 18.7 %collective-permute-start = (f32[2,64,2,128]{3,1,2,0:T(8,128)S(1)}, f32[2,64,2,128]{3,1,2,0:T(8,128)S(1)}, u32[]{:S(2)}, u32[]{:S(2)}) collective-permute-start(f32[2,64,2,128]{3,1,2,0:T(8,128)S(1)} %get-tuple-element.21), channel_id=1, source_target_pairs={{1,0},{2,1},{3,2},{4,3},{5,4},{6,5},{7,6},{8,7},{9,8},{10,9},{11,1... | collective-permute-start | bytes 393224 | tf_op jit(solution)/shard_map/ppermute | solution.py:25
  6.6 16.8 %collective-permute-start.1 = (f32[2,64,2,128]{3,1,2,0:T(8,128)S(1)}, f32[2,64,2,128]{3,1,2,0:T(8,128)S(1)}, u32[]{:S(2)}, u32[]{:S(2)}) collective-permute-start(f32[2,64,2,128]{3,1,2,0:T(8,128)S(1)} %get-tuple-element.22), channel_id=1, source_target_pairs={{0,1},{1,2},{2,3},{3,4},{4,5},{5,6},{6,7},{7,8},{8,9},{9,10},{10,1... | collective-permute-start | bytes 393224 | tf_op jit(solution)/shard_map/ppermute | solution.py:22
  12.0 32.6 %collective-permute-start.3 = (f32[2,64,8,128]{3,1,2,0:T(8,128)S(1)}, f32[2,64,8,128]{3,1,2,0:T(8,128)S(1)}, u32[]{:S(2)}, u32[]{:S(2)}) collective-permute-start(f32[2,64,8,128]{3,1,2,0:T(8,128)S(1)} %fusion.44), channel_id=1, source_target_pairs={{0,128},{128,256},{256,384},{384,512},{512,640},{640,768},{768,896... | collective-permute-start | bytes 1572872 | tf_op jit(solution)/shard_map/ppermute | solution.py:33
  46.6 33.2 %collective-permute-start.6 = (f32[2,64,8,128]{3,1,2,0:T(8,128)S(1)}, f32[2,64,8,128]{3,1,2,0:T(8,128)S(1)}, u32[]{:S(2)}, u32[]{:S(2)}) collective-permute-start(f32[2,64,8,128]{3,1,2,0:T(8,128)S(1)} %pad_maximum_fusion), channel_id=1, source_target_pairs={{128,0},{256,128},{384,256},{512,384},{640,512},{768,640},{896,768... | collective-permute-start | bytes 1572872 | tf_op jit(solution)/shard_map/ppermute | solution.py:33
  48.5 15.9 %collective-permute-start.4 = (f32[2,64,2,128]{3,1,2,0:T(8,128)S(1)}, f32[2,64,2,128]{3,1,2,0:T(8,128)S(1)}, u32[]{:S(2)}, u32[]{:S(2)}) collective-permute-start(f32[2,64,2,128]{3,1,2,0:T(8,128)S(1)} %get-tuple-element.18), channel_id=1, source_target_pairs={{1,0},{2,1},{3,2},{4,3},{5,4},{6,5},{7,6},{8,7},{9,8},{10,9},{11,1... | collective-permute-start | bytes 393224 | tf_op jit(solution)/shard_map/ppermute | solution.py:25
  50.4 14.0 %collective-permute-start.5 = (f32[2,64,2,128]{3,1,2,0:T(8,128)S(1)}, f32[2,64,2,128]{3,1,2,0:T(8,128)S(1)}, u32[]{:S(2)}, u32[]{:S(2)}) collective-permute-start(f32[2,64,2,128]{3,1,2,0:T(8,128)S(1)} %get-tuple-element.17), channel_id=1, source_target_pairs={{0,1},{1,2},{2,3},{3,4},{4,5},{5,6},{6,7},{7,8},{8,9},{9,10},{10,1... | collective-permute-start | bytes 393224 | tf_op jit(solution)/shard_map/ppermute | solution.py:22
  54.4 32.0 %collective-permute-start.7 = (f32[2,64,8,128]{3,1,2,0:T(8,128)S(1)}, f32[2,64,8,128]{3,1,2,0:T(8,128)S(1)}, u32[]{:S(2)}, u32[]{:S(2)}) collective-permute-start(f32[2,64,8,128]{3,1,2,0:T(8,128)S(1)} %fusion.34), channel_id=1, source_target_pairs={{0,128},{128,256},{256,384},{384,512},{512,640},{640,768},{768,896... | collective-permute-start | bytes 1572872 | tf_op jit(solution)/shard_map/ppermute | solution.py:33
  87.8 26.8 %collective-permute-start.10 = (f32[2,64,8,128]{3,1,2,0:T(8,128)S(1)}, f32[2,64,8,128]{3,1,2,0:T(8,128)S(1)}, u32[]{:S(2)}, u32[]{:S(2)}) collective-permute-start(f32[2,64,8,128]{3,1,2,0:T(8,128)S(1)} %fusion.97), channel_id=1, source_target_pairs={{128,0},{256,128},{384,256},{512,384},{640,512},{768,640},{896,768... | collective-permute-start | bytes 1572872 | tf_op jit(solution)/shard_map/ppermute | solution.py:33
  90.4 15.6 %collective-permute-start.8 = (f32[2,64,2,128]{3,1,2,0:T(8,128)S(1)}, f32[2,64,2,128]{3,1,2,0:T(8,128)S(1)}, u32[]{:S(2)}, u32[]{:S(2)}) collective-permute-start(f32[2,64,2,128]{3,1,2,0:T(8,128)S(1)} %get-tuple-element.11), channel_id=1, source_target_pairs={{1,0},{2,1},{3,2},{4,3},{5,4},{6,5},{7,6},{8,7},{9,8},{10,9},{11,1... | collective-permute-start | bytes 393224 | tf_op jit(solution)/shard_map/ppermute | solution.py:25
  92.3 13.6 %collective-permute-start.9 = (f32[2,64,2,128]{3,1,2,0:T(8,128)S(1)}, f32[2,64,2,128]{3,1,2,0:T(8,128)S(1)}, u32[]{:S(2)}, u32[]{:S(2)}) collective-permute-start(f32[2,64,2,128]{3,1,2,0:T(8,128)S(1)} %get-tuple-element.12), channel_id=1, source_target_pairs={{0,1},{1,2},{2,3},{3,4},{4,5},{5,6},{6,7},{7,8},{8,9},{9,10},{10,1... | collective-permute-start | bytes 393224 | tf_op jit(solution)/shard_map/ppermute | solution.py:22
  97.0 31.8 %collective-permute-start.11 = (f32[2,64,8,128]{3,1,2,0:T(8,128)S(1)}, f32[2,64,8,128]{3,1,2,0:T(8,128)S(1)}, u32[]{:S(2)}, u32[]{:S(2)}) collective-permute-start(f32[2,64,8,128]{3,1,2,0:T(8,128)S(1)} %fusion.24), channel_id=1, source_target_pairs={{0,128},{128,256},{256,384},{384,512},{512,640},{640,768},{768,896... | collective-permute-start | bytes 1572872 | tf_op jit(solution)/shard_map/ppermute | solution.py:33
  130.2 25.7 %collective-permute-start.14 = (f32[2,64,8,128]{3,1,2,0:T(8,128)S(1)}, f32[2,64,8,128]{3,1,2,0:T(8,128)S(1)}, u32[]{:S(2)}, u32[]{:S(2)}) collective-permute-start(f32[2,64,8,128]{3,1,2,0:T(8,128)S(1)} %fusion.96), channel_id=1, source_target_pairs={{128,0},{256,128},{384,256},{512,384},{640,512},{768,640},{896,768... | collective-permute-start | bytes 1572872 | tf_op jit(solution)/shard_map/ppermute | solution.py:33
  132.7 21.7 %collective-permute-start.12 = (f32[2,64,2,128]{3,1,2,0:T(8,128)S(1)}, f32[2,64,2,128]{3,1,2,0:T(8,128)S(1)}, u32[]{:S(2)}, u32[]{:S(2)}) collective-permute-start(f32[2,64,2,128]{3,1,2,0:T(8,128)S(1)} %get-tuple-element.7), channel_id=1, source_target_pairs={{1,0},{2,1},{3,2},{4,3},{5,4},{6,5},{7,6},{8,7},{9,8},{10,9},{11,1... | collective-permute-start | bytes 393224 | tf_op jit(solution)/shard_map/ppermute | solution.py:25
  134.7 19.8 %collective-permute-start.13 = (f32[2,64,2,128]{3,1,2,0:T(8,128)S(1)}, f32[2,64,2,128]{3,1,2,0:T(8,128)S(1)}, u32[]{:S(2)}, u32[]{:S(2)}) collective-permute-start(f32[2,64,2,128]{3,1,2,0:T(8,128)S(1)} %get-tuple-element.8), channel_id=1, source_target_pairs={{0,1},{1,2},{2,3},{3,4},{4,5},{5,6},{6,7},{7,8},{8,9},{9,10},{10,1... | collective-permute-start | bytes 393224 | tf_op jit(solution)/shard_map/ppermute | solution.py:22
  139.3 31.6 %collective-permute-start.15 = (f32[2,64,8,128]{3,1,2,0:T(8,128)S(1)}, f32[2,64,8,128]{3,1,2,0:T(8,128)S(1)}, u32[]{:S(2)}, u32[]{:S(2)}) collective-permute-start(f32[2,64,8,128]{3,1,2,0:T(8,128)S(1)} %fusion.14), channel_id=1, source_target_pairs={{0,128},{128,256},{256,384},{384,512},{512,640},{640,768},{768,896... | collective-permute-start | bytes 1572872 | tf_op jit(solution)/shard_map/ppermute | solution.py:33
  156.5 15.1 %copy-start.1 = (f32[2,64,8,128]{3,2,1,0:T(8,128)S(1)}, f32[2,64,8,128]{3,2,1,0:T(8,128)}, u32[]{:S(2)}) copy-start(f32[2,64,8,128]{3,2,1,0:T(8,128)} %param.4) | copy-start | bytes 1572868
where the time goes:
time: 174 us; the launch traced here: 173 us
  waiting for transfers between devices  80.2 us (46%)
  starting transfers between devices  67 us (39%)
  matrix products  18.9 us (11%)
  other arithmetic  5.17 us (3%)
    ppermute x8, waiting for transfers between devices, passed_along(): return lax.ppermute(value, axis, pairs)  73.9 us
    ppermute x8, starting transfers between devices, passed_along(): return lax.ppermute(value, axis, pairs)  45.2 us
    ppermute x4, starting transfers between devices, extended(): lax.ppermute(lax.slice_in_dim(block, block.shape[dim] - width, None, axis...  14.1 us
    dot_general x12, matrix products, local(): jnp.einsum('cd,sdij->scij', coupling[degree], term, precision=highest)  8.78 us
    ppermute x4, starting transfers between devices, extended(): lax.ppermute(lax.slice_in_dim(block, 0, width, axis=dim), axis, backward)  7.68 us
    ppermute x4, waiting for transfers between devices, extended(): lax.ppermute(lax.slice_in_dim(block, 0, width, axis=dim), axis, backward)  6.24 us
  transfers between devices with their start and end apart: 16, of which 9 were waited for; matrix products, arithmetic and copies ran while one was open for 9% of the time, Pallas kernels for 0%

commit v1 on v0

v1 whole, which is shorter than its diff:
```python
import functools

import jax
import jax.numpy as jnp
from jax import lax
from jax.experimental import pallas as pl
from jax.experimental.pallas import tpu as pltpu
from jax.sharding import PartitionSpec as P

ORDER = 4

kinetic_scale = 0.2
coulomb_charge = 4.0
radius_offset = 16.0
center_weight = -2.5
near_weight = 4.0 / 3.0
far_weight = -1.0 / 12.0

near = -kinetic_scale * near_weight
far = -kinetic_scale * far_weight

f32 = jnp.float32
bf16 = jnp.bfloat16


def split_weights(mat):
    rounded = lax.reduce_precision(mat, 8, 7)
    high = rounded.astype(bf16)
    low = (mat - rounded).astype(bf16)
    return jnp.concatenate([high, high, low], axis=1)


def split_field(x):
    high = x.astype(bf16)
    low = (x - high.astype(f32)).astype(bf16)
    return jnp.concatenate([high, low, high], axis=0)


def both(ref, i):
    return jnp.concatenate([ref[0, i], ref[1, i]], axis=1)


def times(weights, x):
    return jnp.dot(weights, split_field(x), preferred_element_type=f32)


def twice(row):
    return jnp.concatenate([row, row], axis=1)


def start_kernel(psi_ref, live_ref, term_ref):
    live = live_ref[...]
    for s in range(2):
        for i in range(term_ref.shape[1]):
            term_ref[s, i] = psi_ref[s, :, i, :] * live


def own_kernel(term_ref, weights_ref, coef_ref, pot_ref, out_ref, low_ref, high_ref):
    rows = term_ref.shape[1]
    slots = term_ref.shape[2]
    lanes = term_ref.shape[3]
    low_ref[...] = term_ref[:, 0:2]
    high_ref[...] = term_ref[:, rows - 2 : rows]
    lane = lax.broadcasted_iota(jnp.int32, (slots, lanes), 1)
    weights = weights_ref[...]
    for i in range(rows):
        mixed = times(weights, both(term_ref, i))
        ratio = twice(coef_ref[i, 0:1])
        mixed = mixed[:slots] + ratio * (mixed[slots : 2 * slots] + ratio * mixed[2 * slots :])
        for s in range(2):
            x = term_ref[s, i]
            acc = mixed[:, s * lanes : (s + 1) * lanes] + pot_ref[i] * x
            close = jnp.where(lane >= 1, pltpu.roll(x, 1, 1), 0.0) + jnp.where(
                lane < lanes - 1, pltpu.roll(x, lanes - 1, 1), 0.0
            )
            wide = jnp.where(lane >= 2, pltpu.roll(x, 2, 1), 0.0) + jnp.where(
                lane < lanes - 2, pltpu.roll(x, lanes - 2, 1), 0.0
            )
            for step in (-1, 1):
                if 0 <= i + step < rows:
                    close = close + term_ref[s, i + step]
                if 0 <= i + 2 * step < rows:
                    wide = wide + term_ref[s, i + 2 * step]
            out_ref[s, i] = acc + near * close + far * wide


def chip_kernel(part_ref, other_ref, weights_ref, coef_ref, below_ref, above_ref, out_ref):
    rows, slots, lanes = out_ref.shape[1:]
    weights = weights_ref[...]
    for i in range(rows):
        mixed = times(weights, both(other_ref, i))
        mixed = twice(coef_ref[i, 1:2]) * mixed[:slots] + twice(coef_ref[i, 2:3]) * mixed[slots:]
        for s in range(2):
            acc = part_ref[s, i] + mixed[:, s * lanes : (s + 1) * lanes]
            if i == 0:
                acc = acc + near * below_ref[s, 1] + far * below_ref[s, 0]
            if i == 1:
                acc = acc + far * below_ref[s, 1]
            if i == rows - 1:
                acc = acc + near * above_ref[s, 0] + far * above_ref[s, 1]
            if i == rows - 2:
                acc = acc + far * above_ref[s, 0]
            out_ref[s, i] = acc


def finish_kernel(order_index, last, part_ref, other_ref, weights_ref, coef_ref, live_ref, total_ref, *outs):
    rows, slots, lanes = part_ref.shape[1:]
    weights = weights_ref[...]
    scale = live_ref[...] / float(order_index)
    for i in range(rows):
        mixed = times(weights, both(other_ref, i))
        mixed = twice(coef_ref[i, 1:2]) * mixed[:slots] + twice(coef_ref[i, 2:3]) * mixed[slots:]
        real = (part_ref[1, i] + mixed[:, lanes:]) * scale
        imag = -((part_ref[0, i] + mixed[:, :lanes]) * scale)
        if last:
            outs[0][0, :, i, :] = total_ref[0, i] + real
            outs[0][1, :, i, :] = total_ref[1, i] + imag
        else:
            outs[0][0, i] = real
            outs[0][1, i] = imag
            outs[1][0, i] = total_ref[0, i] + real
            outs[1][1, i] = total_ref[1, i] + imag


def call(kernel, outs, *args):
    cost = pl.CostEstimate(flops=800_000_000, bytes_accessed=3_000_000, transcendentals=0)
    return pl.pallas_call(
        kernel,
        out_shape=outs,
        cost_estimate=cost,
        compiler_params=pltpu.CompilerParams(vmem_limit_bytes=32 * 1024 * 1024),
    )(*args)


def swaps(count, first):
    found = []
    for i in range(first, count - 1, 2):
        found += [(i, i + 1), (i + 1, i)]
    return found


def shifts(count, by):
    return [(i, i + by) for i in range(count) if 0 <= i + by < count]


def local(psi_in, channels, multipole, dipole):
    _, slots, rows, lanes = psi_in.shape
    blocks = lax.axis_size("lgroup")
    strips = lax.axis_size("row")
    total_rows = strips * rows
    first_row = lax.axis_index("row") * rows
    even = lax.axis_index("lgroup") % 2 == 0

    field = jax.ShapeDtypeStruct((2, rows, slots, lanes), f32)
    edge = jax.ShapeDtypeStruct((2, 2, slots, lanes), f32)
    live = (channels[0, 0, :] >= 0).astype(f32)[:, None]
    live = jnp.broadcast_to(live, (slots, lanes))
    term = call(start_kernel, field, psi_in, live)

    ang_one = channels[0, 0, :].astype(f32)
    ang_two = channels[0, 1, :].astype(f32)
    radius_one = (first_row + jnp.arange(rows)).astype(f32) + radius_offset
    radius_two = jnp.arange(lanes).astype(f32) + radius_offset
    potential = (
        (ang_one * (ang_one + 1.0))[None, :, None] / (radius_one**2)[:, None, None]
        + (ang_two * (ang_two + 1.0))[None, :, None] / (radius_two**2)[None, None, :]
        - coulomb_charge * (1.0 / radius_one[:, None, None] + 1.0 / radius_two[None, None, :])
    ) - kinetic_scale * 2.0 * center_weight
    ratio = jnp.minimum(radius_one[:, None], radius_two[None, :]) / jnp.maximum(
        radius_one[:, None], radius_two[None, :]
    )
    weight_one = jnp.broadcast_to((radius_one / (total_rows + radius_offset))[:, None], (rows, lanes))
    weight_two = jnp.broadcast_to((radius_two / (lanes + radius_offset))[None, :], (rows, lanes))
    coef = jnp.stack([ratio, weight_one, weight_two] + [jnp.zeros_like(ratio)] * 5, axis=1)

    coupling = 0.5 * (multipole[0] + jnp.swapaxes(multipole[0], -1, -2))
    own = split_weights(coupling.reshape(-1, slots))
    lower = lax.ppermute(dipole[0], "lgroup", shifts(blocks, 1))
    upward = dipole[0].reshape(-1, slots)
    downward = jnp.swapaxes(lower, -1, -2).reshape(-1, slots)
    chip_weights = split_weights(jnp.where(even, upward, downward))
    cross_weights = split_weights(jnp.where(even, downward, upward))

    total = term
    for order_index in range(1, ORDER + 1):
        across = lax.ppermute(term, "lgroup", swaps(blocks, 1))
        beside = lax.ppermute(term, "lgroup", swaps(blocks, 0))
        part, low, high = call(own_kernel, (field, edge, edge), term, own, coef, potential)
        below = lax.ppermute(high, "row", shifts(strips, 1))
        above = lax.ppermute(low, "row", shifts(strips, -1))
        part = call(chip_kernel, field, part, beside, chip_weights, coef, below, above)
        last = order_index == ORDER
        outs = jax.ShapeDtypeStruct(psi_in.shape, f32) if last else (field, field)
        done = call(
            functools.partial(finish_kernel, order_index, last),
            outs, part, across, cross_weights, coef, live, total,
        )
        if last:
            return done
        term, total = done


def solution(mesh):
    placed = (
        P(None, "lgroup", "row", None),
        P("lgroup", None, None),
        P("lgroup", None, None, None),
        P("lgroup", None, None, None),
    )
    return jax.shard_map(
        local, mesh=mesh, in_specs=placed, out_specs=P(None, "lgroup", "row", None), check_vma=False
    )
```

time: 174 us -> 162 us (0.931)
  the two profiles are of different devices: /device:TPU:353 before, /device:TPU:262 now
where the time goes in v1:
time: 162 us; the launch traced here: 161 us
  waiting for transfers between devices  75.4 us (47%)
  starting transfers between devices  75.3 us (46%)
  Pallas kernels  6.6 us (4%)
  local copies, waits for them, and re-layouts  2.16 us (1%)
    ppermute x4, waiting for transfers between devices, local(): below = lax.ppermute(high, 'row', shifts(strips, 1))  67.5 us
    ppermute x4, starting transfers between devices, local(): above = lax.ppermute(low, 'row', shifts(strips, -1))  33.3 us
    ppermute x4, starting transfers between devices, local(): beside = lax.ppermute(term, 'lgroup', swaps(blocks, 0))  22.5 us
    ppermute x4, starting transfers between devices, local(): below = lax.ppermute(high, 'row', shifts(strips, 1))  9.87 us
    ppermute x4, waiting for transfers between devices, local(): above = lax.ppermute(low, 'row', shifts(strips, -1))  7.96 us
    ppermute x4, starting transfers between devices, local(): across = lax.ppermute(term, 'lgroup', swaps(blocks, 1))  7.68 us
    pallas_call x13, Pallas kernels, call(): pl.pallas_call(kernel, out_shape=outs, cost_estimate=cost, compiler_param...  6.6 us
  transfers between devices with their start and end apart: 17, of which 5 were waited for; matrix products, arithmetic and copies ran while one was open for 1% of the time, Pallas kernels for 2%

profile of v1, /device:TPU:262, one launch (start us, length us, event | category | flops | bytes accessed | tf_op | source)
XLA Modules:
  0.0 161.3 jit_solution(18339676373886013606)
XLA Ops:
  0.0 0.7 fusion.4
  0.8 1.0 copy-done
  2.1 1.9 %collective-permute-start.4 = (f32[2,8,64,128]{3,2,1,0:T(8,128)S(1)}, f32[2,8,64,128]{3,2,1,0:T(8,128)S(1)}, u32[]{:S(2)}, u32[]{:S(2)}) collective-permute-start(f32[2,8,64,128]{3,2,1,0:T(8,128)S(1)} %shard_map.46.term_ref.total_ref), channel_id=1, source_target_pairs={{128,256},{256,128},{384,512},{512,384},{640,768},{768,640},{129,2... | collective-permute-start | bytes 1572872 | tf_op jit(solution)/shard_map/ppermute | solution.py:186
  4.0 11.0 %collective-permute-start = (f32[2,8,64,128]{3,2,1,0:T(8,128)S(1)}, f32[2,8,64,128]{3,2,1,0:T(8,128)S(1)}, u32[]{:S(2)}, u32[]{:S(2)}) collective-permute-start(f32[2,8,64,128]{3,2,1,0:T(8,128)S(1)} %shard_map.46.term_ref.total_ref), channel_id=1, source_target_pairs={{0,128},{128,0},{256,384},{384,256},{512,640},{640,512},{768,896},... | collective-permute-start | bytes 1572872 | tf_op jit(solution)/shard_map/ppermute | solution.py:187
  15.1 1.9 %collective-permute-start.1 = (f32[2,64,64]{2,1,0:T(8,128)S(1)}, f32[2,64,64]{2,1,0:T(8,128)S(1)}, u32[]{:S(2)}, u32[]{:S(2)}) collective-permute-start(f32[2,64,64]{2,1,0:T(8,128)S(1)} %bitcast.42), channel_id=1, source_target_pairs={{0,128},{128,256},{256,384},{384,512},{512,640},{640,768},{768,896... | collective-permute-start | bytes 98312 | tf_op jit(solution)/shard_map/ppermute | solution.py:178
  17.0 0.7 copy-done.3
  18.6 0.7 shard_map.47
  19.3 3.4 %collective-permute-start.2 = (f32[2,2,64,128]{3,2,1,0:T(8,128)S(1)}, f32[2,2,64,128]{3,2,1,0:T(8,128)S(1)}, u32[]{:S(2)}, u32[]{:S(2)}) collective-permute-start(f32[2,2,64,128]{3,2,1,0:T(8,128)S(1)} %get-tuple-element.24), channel_id=1, source_target_pairs={{0,1},{1,2},{2,3},{3,4},{4,5},{5,6},{6,7},{7,8},{8,9},{9,10},{10,1... | collective-permute-start | bytes 393224 | tf_op jit(solution)/shard_map/ppermute | solution.py:189
  22.7 7.3 %collective-permute-start.3 = (f32[2,2,64,128]{3,2,1,0:T(8,128)S(1)}, f32[2,2,64,128]{3,2,1,0:T(8,128)S(1)}, u32[]{:S(2)}, u32[]{:S(2)}) collective-permute-start(f32[2,2,64,128]{3,2,1,0:T(8,128)S(1)} %get-tuple-element.25), channel_id=1, source_target_pairs={{1,0},{2,1},{3,2},{4,3},{5,4},{6,5},{7,6},{8,7},{9,8},{10,9},{11,1... | collective-permute-start | bytes 393224 | tf_op jit(solution)/shard_map/ppermute | solution.py:190
  30.2 12.8 %collective-permute-done.2.below_ref = f32[2,2,64,128]{3,2,1,0:T(8,128)S(1)} collective-permute-done((f32[2,2,64,128]{3,2,1,0:T(8,128)S(1)}, f32[2,2,64,128]{3,2,1,0:T(8,128)S(1)}, u32[]{:S(2)}, u32[]{:S(2)}) %collective-permute-start.2) | collective-permute-done | bytes 131104 | tf_op jit(solution)/shard_map/ppermute | solution.py:189
  43.6 3.3 %collective-permute-start.5 = (f32[2,8,64,128]{3,2,1,0:T(8,128)S(1)}, f32[2,8,64,128]{3,2,1,0:T(8,128)S(1)}, u32[]{:S(2)}, u32[]{:S(2)}) collective-permute-start(f32[2,8,64,128]{3,2,1,0:T(8,128)S(1)} %get-tuple-element.26.term_ref), channel_id=1, source_target_pairs={{0,128},{128,0},{256,384},{384,256},{512,640},{640,512},{768,896},... | collective-permute-start | bytes 1572872 | tf_op jit(solution)/shard_map/ppermute | solution.py:187
  46.9 1.9 %collective-permute-start.8 = (f32[2,8,64,128]{3,2,1,0:T(8,128)S(1)}, f32[2,8,64,128]{3,2,1,0:T(8,128)S(1)}, u32[]{:S(2)}, u32[]{:S(2)}) collective-permute-start(f32[2,8,64,128]{3,2,1,0:T(8,128)S(1)} %get-tuple-element.26.term_ref), channel_id=1, source_target_pairs={{128,256},{256,128},{384,512},{512,384},{640,768},{768,640},{129,2... | collective-permute-start | bytes 1572872 | tf_op jit(solution)/shard_map/ppermute | solution.py:186
  48.9 0.7 shard_map.50
  49.6 2.6 %collective-permute-start.6 = (f32[2,2,64,128]{3,2,1,0:T(8,128)S(1)}, f32[2,2,64,128]{3,2,1,0:T(8,128)S(1)}, u32[]{:S(2)}, u32[]{:S(2)}) collective-permute-start(f32[2,2,64,128]{3,2,1,0:T(8,128)S(1)} %get-tuple-element.28), channel_id=1, source_target_pairs={{0,1},{1,2},{2,3},{3,4},{4,5},{5,6},{6,7},{7,8},{8,9},{9,10},{10,1... | collective-permute-start | bytes 393224 | tf_op jit(solution)/shard_map/ppermute | solution.py:189
  52.2 8.6 %collective-permute-start.7 = (f32[2,2,64,128]{3,2,1,0:T(8,128)S(1)}, f32[2,2,64,128]{3,2,1,0:T(8,128)S(1)}, u32[]{:S(2)}, u32[]{:S(2)}) collective-permute-start(f32[2,2,64,128]{3,2,1,0:T(8,128)S(1)} %get-tuple-element.29), channel_id=1, source_target_pairs={{1,0},{2,1},{3,2},{4,3},{5,4},{6,5},{7,6},{8,7},{9,8},{10,9},{11,1... | collective-permute-start | bytes 393224 | tf_op jit(solution)/shard_map/ppermute | solution.py:190
  60.8 23.8 %collective-permute-done.6.below_ref = f32[2,2,64,128]{3,2,1,0:T(8,128)S(1)} collective-permute-done((f32[2,2,64,128]{3,2,1,0:T(8,128)S(1)}, f32[2,2,64,128]{3,2,1,0:T(8,128)S(1)}, u32[]{:S(2)}, u32[]{:S(2)}) %collective-permute-start.6) | collective-permute-done | bytes 131104 | tf_op jit(solution)/shard_map/ppermute | solution.py:189
  84.9 0.3 shard_map.52
  85.2 1.9 %collective-permute-start.9 = (f32[2,8,64,128]{3,2,1,0:T(8,128)S(1)}, f32[2,8,64,128]{3,2,1,0:T(8,128)S(1)}, u32[]{:S(2)}, u32[]{:S(2)}) collective-permute-start(f32[2,8,64,128]{3,2,1,0:T(8,128)S(1)} %get-tuple-element.31.term_ref), channel_id=1, source_target_pairs={{0,128},{128,0},{256,384},{384,256},{512,640},{640,512},{768,896},... | collective-permute-start | bytes 1572872 | tf_op jit(solution)/shard_map/ppermute | solution.py:187
  87.1 1.9 %collective-permute-start.12 = (f32[2,8,64,128]{3,2,1,0:T(8,128)S(1)}, f32[2,8,64,128]{3,2,1,0:T(8,128)S(1)}, u32[]{:S(2)}, u32[]{:S(2)}) collective-permute-start(f32[2,8,64,128]{3,2,1,0:T(8,128)S(1)} %get-tuple-element.31.term_ref), channel_id=1, source_target_pairs={{128,256},{256,128},{384,512},{512,384},{640,768},{768,640},{129,2... | collective-permute-start | bytes 1572872 | tf_op jit(solution)/shard_map/ppermute | solution.py:186
  89.1 0.7 shard_map.53
  89.8 1.9 %collective-permute-start.10 = (f32[2,2,64,128]{3,2,1,0:T(8,128)S(1)}, f32[2,2,64,128]{3,2,1,0:T(8,128)S(1)}, u32[]{:S(2)}, u32[]{:S(2)}) collective-permute-start(f32[2,2,64,128]{3,2,1,0:T(8,128)S(1)} %get-tuple-element.33), channel_id=1, source_target_pairs={{0,1},{1,2},{2,3},{3,4},{4,5},{5,6},{6,7},{7,8},{8,9},{9,10},{10,1... | collective-permute-start | bytes 393224 | tf_op jit(solution)/shard_map/ppermute | solution.py:189
  91.7 8.7 %collective-permute-start.11 = (f32[2,2,64,128]{3,2,1,0:T(8,128)S(1)}, f32[2,2,64,128]{3,2,1,0:T(8,128)S(1)}, u32[]{:S(2)}, u32[]{:S(2)}) collective-permute-start(f32[2,2,64,128]{3,2,1,0:T(8,128)S(1)} %get-tuple-element.34), channel_id=1, source_target_pairs={{1,0},{2,1},{3,2},{4,3},{5,4},{6,5},{7,6},{8,7},{9,8},{10,9},{11,1... | collective-permute-start | bytes 393224 | tf_op jit(solution)/shard_map/ppermute | solution.py:190
  100.4 7.6 %collective-permute-done.10.below_ref = f32[2,2,64,128]{3,2,1,0:T(8,128)S(1)} collective-permute-done((f32[2,2,64,128]{3,2,1,0:T(8,128)S(1)}, f32[2,2,64,128]{3,2,1,0:T(8,128)S(1)}, u32[]{:S(2)}, u32[]{:S(2)}) %collective-permute-start.10) | collective-permute-done | bytes 131104 | tf_op jit(solution)/shard_map/ppermute | solution.py:189
  108.1 7.9 %collective-permute-done.11.above_ref = f32[2,2,64,128]{3,2,1,0:T(8,128)S(1)} collective-permute-done((f32[2,2,64,128]{3,2,1,0:T(8,128)S(1)}, f32[2,2,64,128]{3,2,1,0:T(8,128)S(1)}, u32[]{:S(2)}, u32[]{:S(2)}) %collective-permute-start.11) | collective-permute-done | bytes 131104 | tf_op jit(solution)/shard_map/ppermute | solution.py:190
  116.3 0.3 shard_map.55
  116.7 6.3 %collective-permute-start.13 = (f32[2,8,64,128]{3,2,1,0:T(8,128)S(1)}, f32[2,8,64,128]{3,2,1,0:T(8,128)S(1)}, u32[]{:S(2)}, u32[]{:S(2)}) collective-permute-start(f32[2,8,64,128]{3,2,1,0:T(8,128)S(1)} %get-tuple-element.36.term_ref), channel_id=1, source_target_pairs={{0,128},{128,0},{256,384},{384,256},{512,640},{640,512},{768,896},... | collective-permute-start | bytes 1572872 | tf_op jit(solution)/shard_map/ppermute | solution.py:187
  123.0 1.9 %collective-permute-start.16 = (f32[2,8,64,128]{3,2,1,0:T(8,128)S(1)}, f32[2,8,64,128]{3,2,1,0:T(8,128)S(1)}, u32[]{:S(2)}, u32[]{:S(2)}) collective-permute-start(f32[2,8,64,128]{3,2,1,0:T(8,128)S(1)} %get-tuple-element.36.term_ref), channel_id=1, source_target_pairs={{128,256},{256,128},{384,512},{512,384},{640,768},{768,640},{129,2... | collective-permute-start | bytes 1572872 | tf_op jit(solution)/shard_map/ppermute | solution.py:186
  124.9 0.7 shard_map.56
  125.6 1.9 %collective-permute-start.14 = (f32[2,2,64,128]{3,2,1,0:T(8,128)S(1)}, f32[2,2,64,128]{3,2,1,0:T(8,128)S(1)}, u32[]{:S(2)}, u32[]{:S(2)}) collective-permute-start(f32[2,2,64,128]{3,2,1,0:T(8,128)S(1)} %get-tuple-element.38), channel_id=1, source_target_pairs={{0,1},{1,2},{2,3},{3,4},{4,5},{5,6},{6,7},{7,8},{8,9},{9,10},{10,1... | collective-permute-start | bytes 393224 | tf_op jit(solution)/shard_map/ppermute | solution.py:189
  127.5 8.7 %collective-permute-start.15 = (f32[2,2,64,128]{3,2,1,0:T(8,128)S(1)}, f32[2,2,64,128]{3,2,1,0:T(8,128)S(1)}, u32[]{:S(2)}, u32[]{:S(2)}) collective-permute-start(f32[2,2,64,128]{3,2,1,0:T(8,128)S(1)} %get-tuple-element.39), channel_id=1, source_target_pairs={{1,0},{2,1},{3,2},{4,3},{5,4},{6,5},{7,6},{8,7},{9,8},{10,9},{11,1... | collective-permute-start | bytes 393224 | tf_op jit(solution)/shard_map/ppermute | solution.py:190
  136.3 23.3 %collective-permute-done.14.below_ref = f32[2,2,64,128]{3,2,1,0:T(8,128)S(1)} collective-permute-done((f32[2,2,64,128]{3,2,1,0:T(8,128)S(1)}, f32[2,2,64,128]{3,2,1,0:T(8,128)S(1)}, u32[]{:S(2)}, u32[]{:S(2)}) %collective-permute-start.14) | collective-permute-done | bytes 131104 | tf_op jit(solution)/shard_map/ppermute | solution.py:189
  159.9 1.4 shard_map.58
  (50 shorter events, 3.0 us)
Async XLA Ops:
  0.8 1.0 copy-start
  1.8 13.2 %copy-start.2 = (f32[1,2,64,64]{3,2,1,0:T(8,128)S(1)}, f32[1,2,64,64]{3,2,1,0:T(8,128)}, u32[]{:S(2)}) copy-start(f32[1,2,64,64]{3,2,1,0:T(8,128)} %param.7) | copy-start | bytes 98308
  1.8 15.9 %copy-start.1 = (f32[1,3,64,64]{3,2,1,0:T(8,128)S(1)}, f32[1,3,64,64]{3,2,1,0:T(8,128)}, u32[]{:S(2)}) copy-start(f32[1,3,64,64]{3,2,1,0:T(8,128)} %param.6) | copy-start | bytes 147460
  2.1 41.2 %collective-permute-start.4 = (f32[2,8,64,128]{3,2,1,0:T(8,128)S(1)}, f32[2,8,64,128]{3,2,1,0:T(8,128)S(1)}, u32[]{:S(2)}, u32[]{:S(2)}) collective-permute-start(f32[2,8,64,128]{3,2,1,0:T(8,128)S(1)} %shard_map.46.term_ref.total_ref), channel_id=1, source_target_pairs={{128,256},{256,128},{384,512},{512,384},{640,768},{768,640},{129,2... | collective-permute-start | bytes 1572872 | tf_op jit(solution)/shard_map/ppermute | solution.py:186
  4.0 39.0 %collective-permute-start = (f32[2,8,64,128]{3,2,1,0:T(8,128)S(1)}, f32[2,8,64,128]{3,2,1,0:T(8,128)S(1)}, u32[]{:S(2)}, u32[]{:S(2)}) collective-permute-start(f32[2,8,64,128]{3,2,1,0:T(8,128)S(1)} %shard_map.46.term_ref.total_ref), channel_id=1, source_target_pairs={{0,128},{128,0},{256,384},{384,256},{512,640},{640,512},{768,896},... | collective-permute-start | bytes 1572872 | tf_op jit(solution)/shard_map/ppermute | solution.py:187
  15.1 14.9 %collective-permute-start.1 = (f32[2,64,64]{2,1,0:T(8,128)S(1)}, f32[2,64,64]{2,1,0:T(8,128)S(1)}, u32[]{:S(2)}, u32[]{:S(2)}) collective-permute-start(f32[2,64,64]{2,1,0:T(8,128)S(1)} %bitcast.42), channel_id=1, source_target_pairs={{0,128},{128,256},{256,384},{384,512},{512,640},{640,768},{768,896... | collective-permute-start | bytes 98312 | tf_op jit(solution)/shard_map/ppermute | solution.py:178
  17.0 0.7 copy-start.3
  19.3 23.7 %collective-permute-start.2 = (f32[2,2,64,128]{3,2,1,0:T(8,128)S(1)}, f32[2,2,64,128]{3,2,1,0:T(8,128)S(1)}, u32[]{:S(2)}, u32[]{:S(2)}) collective-permute-start(f32[2,2,64,128]{3,2,1,0:T(8,128)S(1)} %get-tuple-element.24), channel_id=1, source_target_pairs={{0,1},{1,2},{2,3},{3,4},{4,5},{5,6},{6,7},{7,8},{8,9},{9,10},{10,1... | collective-permute-start | bytes 393224 | tf_op jit(solution)/shard_map/ppermute | solution.py:189
  22.7 20.3 %collective-permute-start.3 = (f32[2,2,64,128]{3,2,1,0:T(8,128)S(1)}, f32[2,2,64,128]{3,2,1,0:T(8,128)S(1)}, u32[]{:S(2)}, u32[]{:S(2)}) collective-permute-start(f32[2,2,64,128]{3,2,1,0:T(8,128)S(1)} %get-tuple-element.25), channel_id=1, source_target_pairs={{1,0},{2,1},{3,2},{4,3},{5,4},{6,5},{7,6},{8,7},{9,8},{10,9},{11,1... | collective-permute-start | bytes 393224 | tf_op jit(solution)/shard_map/ppermute | solution.py:190
  43.6 40.9 %collective-permute-start.5 = (f32[2,8,64,128]{3,2,1,0:T(8,128)S(1)}, f32[2,8,64,128]{3,2,1,0:T(8,128)S(1)}, u32[]{:S(2)}, u32[]{:S(2)}) collective-permute-start(f32[2,8,64,128]{3,2,1,0:T(8,128)S(1)} %get-tuple-element.26.term_ref), channel_id=1, source_target_pairs={{0,128},{128,0},{256,384},{384,256},{512,640},{640,512},{768,896},... | collective-permute-start | bytes 1572872 | tf_op jit(solution)/shard_map/ppermute | solution.py:187
  46.9 38.0 %collective-permute-start.8 = (f32[2,8,64,128]{3,2,1,0:T(8,128)S(1)}, f32[2,8,64,128]{3,2,1,0:T(8,128)S(1)}, u32[]{:S(2)}, u32[]{:S(2)}) collective-permute-start(f32[2,8,64,128]{3,2,1,0:T(8,128)S(1)} %get-tuple-element.26.term_ref), channel_id=1, source_target_pairs={{128,256},{256,128},{384,512},{512,384},{640,768},{768,640},{129,2... | collective-permute-start | bytes 1572872 | tf_op jit(solution)/shard_map/ppermute | solution.py:186
  49.6 35.0 %collective-permute-start.6 = (f32[2,2,64,128]{3,2,1,0:T(8,128)S(1)}, f32[2,2,64,128]{3,2,1,0:T(8,128)S(1)}, u32[]{:S(2)}, u32[]{:S(2)}) collective-permute-start(f32[2,2,64,128]{3,2,1,0:T(8,128)S(1)} %get-tuple-element.28), channel_id=1, source_target_pairs={{0,1},{1,2},{2,3},{3,4},{4,5},{5,6},{6,7},{7,8},{8,9},{9,10},{10,1... | collective-permute-start | bytes 393224 | tf_op jit(solution)/shard_map/ppermute | solution.py:189
  52.2 32.4 %collective-permute-start.7 = (f32[2,2,64,128]{3,2,1,0:T(8,128)S(1)}, f32[2,2,64,128]{3,2,1,0:T(8,128)S(1)}, u32[]{:S(2)}, u32[]{:S(2)}) collective-permute-start(f32[2,2,64,128]{3,2,1,0:T(8,128)S(1)} %get-tuple-element.29), channel_id=1, source_target_pairs={{1,0},{2,1},{3,2},{4,3},{5,4},{6,5},{7,6},{8,7},{9,8},{10,9},{11,1... | collective-permute-start | bytes 393224 | tf_op jit(solution)/shard_map/ppermute | solution.py:190
  85.2 30.8 %collective-permute-start.9 = (f32[2,8,64,128]{3,2,1,0:T(8,128)S(1)}, f32[2,8,64,128]{3,2,1,0:T(8,128)S(1)}, u32[]{:S(2)}, u32[]{:S(2)}) collective-permute-start(f32[2,8,64,128]{3,2,1,0:T(8,128)S(1)} %get-tuple-element.31.term_ref), channel_id=1, source_target_pairs={{0,128},{128,0},{256,384},{384,256},{512,640},{640,512},{768,896},... | collective-permute-start | bytes 1572872 | tf_op jit(solution)/shard_map/ppermute | solution.py:187
  87.1 29.2 %collective-permute-start.12 = (f32[2,8,64,128]{3,2,1,0:T(8,128)S(1)}, f32[2,8,64,128]{3,2,1,0:T(8,128)S(1)}, u32[]{:S(2)}, u32[]{:S(2)}) collective-permute-start(f32[2,8,64,128]{3,2,1,0:T(8,128)S(1)} %get-tuple-element.31.term_ref), channel_id=1, source_target_pairs={{128,256},{256,128},{384,512},{512,384},{640,768},{768,640},{129,2... | collective-permute-start | bytes 1572872 | tf_op jit(solution)/shard_map/ppermute | solution.py:186
  89.8 18.3 %collective-permute-start.10 = (f32[2,2,64,128]{3,2,1,0:T(8,128)S(1)}, f32[2,2,64,128]{3,2,1,0:T(8,128)S(1)}, u32[]{:S(2)}, u32[]{:S(2)}) collective-permute-start(f32[2,2,64,128]{3,2,1,0:T(8,128)S(1)} %get-tuple-element.33), channel_id=1, source_target_pairs={{0,1},{1,2},{2,3},{3,4},{4,5},{5,6},{6,7},{7,8},{8,9},{9,10},{10,1... | collective-permute-start | bytes 393224 | tf_op jit(solution)/shard_map/ppermute | solution.py:189
  91.7 24.3 %collective-permute-start.11 = (f32[2,2,64,128]{3,2,1,0:T(8,128)S(1)}, f32[2,2,64,128]{3,2,1,0:T(8,128)S(1)}, u32[]{:S(2)}, u32[]{:S(2)}) collective-permute-start(f32[2,2,64,128]{3,2,1,0:T(8,128)S(1)} %get-tuple-element.34), channel_id=1, source_target_pairs={{1,0},{2,1},{3,2},{4,3},{5,4},{6,5},{7,6},{8,7},{9,8},{10,9},{11,1... | collective-permute-start | bytes 393224 | tf_op jit(solution)/shard_map/ppermute | solution.py:190
  116.7 42.9 %collective-permute-start.13 = (f32[2,8,64,128]{3,2,1,0:T(8,128)S(1)}, f32[2,8,64,128]{3,2,1,0:T(8,128)S(1)}, u32[]{:S(2)}, u32[]{:S(2)}) collective-permute-start(f32[2,8,64,128]{3,2,1,0:T(8,128)S(1)} %get-tuple-element.36.term_ref), channel_id=1, source_target_pairs={{0,128},{128,0},{256,384},{384,256},{512,640},{640,512},{768,896},... | collective-permute-start | bytes 1572872 | tf_op jit(solution)/shard_map/ppermute | solution.py:187
  123.0 36.9 %collective-permute-start.16 = (f32[2,8,64,128]{3,2,1,0:T(8,128)S(1)}, f32[2,8,64,128]{3,2,1,0:T(8,128)S(1)}, u32[]{:S(2)}, u32[]{:S(2)}) collective-permute-start(f32[2,8,64,128]{3,2,1,0:T(8,128)S(1)} %get-tuple-element.36.term_ref), channel_id=1, source_target_pairs={{128,256},{256,128},{384,512},{512,384},{640,768},{768,640},{129,2... | collective-permute-start | bytes 1572872 | tf_op jit(solution)/shard_map/ppermute | solution.py:186
  125.6 33.9 %collective-permute-start.14 = (f32[2,2,64,128]{3,2,1,0:T(8,128)S(1)}, f32[2,2,64,128]{3,2,1,0:T(8,128)S(1)}, u32[]{:S(2)}, u32[]{:S(2)}) collective-permute-start(f32[2,2,64,128]{3,2,1,0:T(8,128)S(1)} %get-tuple-element.38), channel_id=1, source_target_pairs={{0,1},{1,2},{2,3},{3,4},{4,5},{5,6},{6,7},{7,8},{8,9},{9,10},{10,1... | collective-permute-start | bytes 393224 | tf_op jit(solution)/shard_map/ppermute | solution.py:189
  127.5 32.0 %collective-permute-start.15 = (f32[2,2,64,128]{3,2,1,0:T(8,128)S(1)}, f32[2,2,64,128]{3,2,1,0:T(8,128)S(1)}, u32[]{:S(2)}, u32[]{:S(2)}) collective-permute-start(f32[2,2,64,128]{3,2,1,0:T(8,128)S(1)} %get-tuple-element.39), channel_id=1, source_target_pairs={{1,0},{2,1},{3,2},{4,3},{5,4},{6,5},{7,6},{8,7},{9,8},{10,9},{11,1... | collective-permute-start | bytes 393224 | tf_op jit(solution)/shard_map/ppermute | solution.py:190

commit v2 on v1

--- a/solution.py
+++ b/solution.py
@@ -48,23 +48,32 @@
     return jnp.concatenate([row, row], axis=1)
 
 
-def start_kernel(psi_ref, live_ref, term_ref):
+def start_kernel(psi_ref, live_ref, term_ref, low_ref, high_ref):
     live = live_ref[...]
+    rows = term_ref.shape[1]
     for s in range(2):
-        for i in range(term_ref.shape[1]):
+        for i in range(rows):
             term_ref[s, i] = psi_ref[s, :, i, :] * live
-
-
-def own_kernel(term_ref, weights_ref, coef_ref, pot_ref, out_ref, low_ref, high_ref):
+    low_ref[...] = term_ref[:, 0:2]
+    high_ref[...] = term_ref[:, rows - 2 : rows]
+
+
+def own_kernel(term_ref, weights_ref, sent_ref, coef_ref, pot_ref, out_ref, copy_ref, message_ref):
+    copy_ref[...] = term_ref[...]
+    kept = message_ref.shape[2]
     rows = term_ref.shape[1]
     slots = term_ref.shape[2]
     lanes = term_ref.shape[3]
-    low_ref[...] = term_ref[:, 0:2]
-    high_ref[...] = term_ref[:, rows - 2 : rows]
     lane = lax.broadcasted_iota(jnp.int32, (slots, lanes), 1)
     weights = weights_ref[...]
     for i in range(rows):
-        mixed = times(weights, both(term_ref, i))
+        here = both(term_ref, i)
+        sent = times(sent_ref[...], here)
+        sent = twice(coef_ref[i, 1:2]) * sent[:kept] + twice(coef_ref[i, 2:3]) * sent[slots : slots + kept]
+        sent = twice(coef_ref[i, 3:4]) * here[:kept] + twice(coef_ref[i, 4:5]) * sent
+        for s in range(2):
+            message_ref[s, i] = sent[:, s * lanes : (s + 1) * lanes]
+        mixed = times(weights, here)
         ratio = twice(coef_ref[i, 0:1])
         mixed = mixed[:slots] + ratio * (mixed[slots : 2 * slots] + ratio * mixed[2 * slots :])
         for s in range(2):
@@ -84,12 +93,22 @@
             out_ref[s, i] = acc + near * close + far * wide
 
 
-def chip_kernel(part_ref, other_ref, weights_ref, coef_ref, below_ref, above_ref, out_ref):
-    rows, slots, lanes = out_ref.shape[1:]
-    weights = weights_ref[...]
+def finish_kernel(
+    order_index, last, part_ref, across_ref, beside_ref, below_ref, above_ref,
+    cross_ref, chip_ref, coef_ref, live_ref, total_ref, *outs
+):
+    rows, slots, lanes = part_ref.shape[1:]
+    kept = across_ref.shape[2]
+    scale = live_ref[...] / float(order_index)
     for i in range(rows):
-        mixed = times(weights, both(other_ref, i))
+        came = both(across_ref, i)
+        if kept < slots:
+            came = jnp.concatenate([came, jnp.zeros((slots - kept, 2 * lanes), f32)], axis=0)
+        raw = came * twice(coef_ref[i, 4:5])
+        mixed = times(cross_ref[...], raw) + times(chip_ref[...], both(beside_ref, i))
         mixed = twice(coef_ref[i, 1:2]) * mixed[:slots] + twice(coef_ref[i, 2:3]) * mixed[slots:]
+        mixed = mixed + came * twice(coef_ref[i, 3:4])
+        image = []
         for s in range(2):
             acc = part_ref[s, i] + mixed[:, s * lanes : (s + 1) * lanes]
             if i == 0:
@@ -100,26 +119,19 @@
                 acc = acc + near * above_ref[s, 0] + far * above_ref[s, 1]
             if i == rows - 2:
                 acc = acc + far * above_ref[s, 0]
-            out_ref[s, i] = acc
-
-
-def finish_kernel(order_index, last, part_ref, other_ref, weights_ref, coef_ref, live_ref, total_ref, *outs):
-    rows, slots, lanes = part_ref.shape[1:]
-    weights = weights_ref[...]
-    scale = live_ref[...] / float(order_index)
-    for i in range(rows):
-        mixed = times(weights, both(other_ref, i))
-        mixed = twice(coef_ref[i, 1:2]) * mixed[:slots] + twice(coef_ref[i, 2:3]) * mixed[slots:]
-        real = (part_ref[1, i] + mixed[:, lanes:]) * scale
-        imag = -((part_ref[0, i] + mixed[:, :lanes]) * scale)
+            image.append(acc * scale)
+        real, imag = image[1], -image[0]
         if last:
             outs[0][0, :, i, :] = total_ref[0, i] + real
             outs[0][1, :, i, :] = total_ref[1, i] + imag
-        else:
-            outs[0][0, i] = real
-            outs[0][1, i] = imag
-            outs[1][0, i] = total_ref[0, i] + real
-            outs[1][1, i] = total_ref[1, i] + imag
+            continue
+        for s, value in enumerate((real, imag)):
+            outs[0][s, i] = value
+            outs[1][s, i] = total_ref[s, i] + value
+            if i < 2:
+                outs[2][s, i] = value
+            if i >= rows - 2:
+                outs[3][s, i - (rows - 2)] = value
 
 
 def call(kernel, outs, *args):
@@ -155,7 +167,7 @@
     edge = jax.ShapeDtypeStruct((2, 2, slots, lanes), f32)
     live = (channels[0, 0, :] >= 0).astype(f32)[:, None]
     live = jnp.broadcast_to(live, (slots, lanes))
-    term = call(start_kernel, field, psi_in, live)
+    term, low, high = call(start_kernel, (field, edge, edge), psi_in, live)
 
     ang_one = channels[0, 0, :].astype(f32)
     ang_two = channels[0, 1, :].astype(f32)
@@ -171,7 +183,19 @@
     )
     weight_one = jnp.broadcast_to((radius_one / (total_rows + radius_offset))[:, None], (rows, lanes))
     weight_two = jnp.broadcast_to((radius_two / (lanes + radius_offset))[None, :], (rows, lanes))
-    coef = jnp.stack([ratio, weight_one, weight_two] + [jnp.zeros_like(ratio)] * 5, axis=1)
+
+    alive = jnp.sum(channels[0, 0, :] >= 0).astype(f32)
+    counts = lax.all_to_all(jnp.full((blocks, 8, 128), alive), "lgroup", 0, 0)[:, 0, 0]
+    most = jnp.max(jnp.minimum(counts[1 : blocks - 1 : 2], counts[2:blocks:2])).astype(jnp.int32)
+    place = lax.axis_index("lgroup")
+    facing = jnp.clip(jnp.where(even, place - 1, place + 1), 0, blocks - 1)
+    theirs = jnp.sum(jnp.where(jnp.arange(blocks) == facing, counts, 0.0))
+    fewer = jnp.where(even, alive < theirs, alive <= theirs)
+
+    def coefficients(small):
+        small = jnp.broadcast_to(small.astype(f32), (rows, lanes))
+        spare = [jnp.zeros_like(ratio)] * 3
+        return jnp.stack([ratio, weight_one, weight_two, small, 1.0 - small] + spare, axis=1)
 
     coupling = 0.5 * (multipole[0] + jnp.swapaxes(multipole[0], -1, -2))
     own = split_weights(coupling.reshape(-1, slots))
@@ -180,24 +204,40 @@
     downward = jnp.swapaxes(lower, -1, -2).reshape(-1, slots)
     chip_weights = split_weights(jnp.where(even, upward, downward))
     cross_weights = split_weights(jnp.where(even, downward, upward))
-
-    total = term
-    for order_index in range(1, ORDER + 1):
-        across = lax.ppermute(term, "lgroup", swaps(blocks, 1))
-        beside = lax.ppermute(term, "lgroup", swaps(blocks, 0))
-        part, low, high = call(own_kernel, (field, edge, edge), term, own, coef, potential)
+    onward = jnp.swapaxes(dipole[0], -1, -2).reshape(-1, slots)
+    sent_weights = split_weights(jnp.where(even, lower.reshape(-1, slots), onward))
+
+    def apply(order_index, coef, roles, sent_by, kept, state):
+        term, total, low, high = state
+        message = jax.ShapeDtypeStruct((2, rows, kept, lanes), f32)
+        part, copied, message = call(
+            own_kernel, (field, field, message), term, own, sent_by, coef, potential
+        )
+        across = lax.ppermute(message, "lgroup", swaps(blocks, 1))
+        beside = lax.ppermute(copied, "lgroup", swaps(blocks, 0))
         below = lax.ppermute(high, "row", shifts(strips, 1))
         above = lax.ppermute(low, "row", shifts(strips, -1))
-        part = call(chip_kernel, field, part, beside, chip_weights, coef, below, above)
         last = order_index == ORDER
-        outs = jax.ShapeDtypeStruct(psi_in.shape, f32) if last else (field, field)
-        done = call(
+        outs = jax.ShapeDtypeStruct(psi_in.shape, f32) if last else (field, field, edge, edge)
+        return call(
             functools.partial(finish_kernel, order_index, last),
-            outs, part, across, cross_weights, coef, live, total,
+            outs, part, across, beside, below, above, cross_weights, chip_weights, roles, live, total,
         )
-        if last:
-            return done
-        term, total = done
+
+    def rest(kept):
+        def run(roles, state):
+            for order_index in range(2, ORDER + 1):
+                state = apply(order_index, roles, roles, sent_weights, kept, state)
+            return state
+
+        return run
+
+    everyone = jnp.bool_(True)
+    first = (term, term, low, high)
+    state = apply(1, coefficients(everyone), coefficients(~everyone), own[: 2 * slots], slots, first)
+    sizes = list(range(24, slots, 8)) + [slots]
+    chosen = jnp.sum(most > jnp.asarray(sizes[:-1], jnp.int32)).astype(jnp.int32)
+    return lax.switch(chosen, [rest(kept) for kept in sizes], coefficients(fewer), state)
 
 
 def solution(mesh):

time: 162 us -> 165 us (1.019)
  waiting for transfers between devices: 75.4 us -> 52.7 us
  starting transfers between devices: 75.3 us -> 86.9 us
  local copies, waits for them, and re-layouts: 2.16 us -> 8.96 us
  other arithmetic: 1.37 us -> 5.59 us
  between operations: 0.42 us -> 3.56 us
    ppermute x16, waiting for transfers between devices: 75.4 us -> 52.7 us  [the longest x4 45 us: apply(): below = lax.ppermute(high, 'row', shifts(strips, 1))]
    all_to_all x0 -> x1, starting transfers between devices: none -> 15.6 us  [local(): lax.all_to_all(jnp.full((blocks, 8, 128), alive), 'lgroup', 0, 0)[:, 0, 0]]
    ppermute x16, starting transfers between devices: 73.4 us -> 69.2 us  [the longest x4 33.5 us: apply(): above = lax.ppermute(low, 'row', shifts(strips, -1))]
    unnamed x8 -> x30, local copies, waits for them, and re-layouts: 1.72 us -> 5.4 us
    reduce_sum x0 -> x3, other arithmetic: none -> 2.65 us  [the longest x1 1.35 us: local(): alive = jnp.sum(channels[0, 0, :] >= 0).astype(f32)]
    pallas_call x13 -> x9, Pallas kernels: 6.6 us -> 5.5 us  [call(): pl.pallas_call(kernel, out_shape=outs, cost_estimate=cost, compiler_param...]
  transfers between devices with their start and end apart: 17 -> 18, of which waited for: 5 -> 4; matrix products, arithmetic and copies ran while one was open for 1% -> 4% of each run, Pallas kernels for 2% -> 1%
where the time goes in v2:
time: 165 us; the launch traced here: 164 us
  starting transfers between devices  86.9 us (53%)
  waiting for transfers between devices  52.7 us (32%)
  local copies, waits for them, and re-layouts  8.96 us (5%)
  other arithmetic  5.59 us (3%)
  Pallas kernels  5.5 us (3%)
  between operations  3.56 us (2%)
    ppermute x4, waiting for transfers between devices, apply(): below = lax.ppermute(high, 'row', shifts(strips, 1))  45 us
    ppermute x4, starting transfers between devices, apply(): above = lax.ppermute(low, 'row', shifts(strips, -1))  33.5 us
    all_to_all x1, starting transfers between devices, local(): lax.all_to_all(jnp.full((blocks, 8, 128), alive), 'lgroup', 0, 0)[:, 0, 0]  15.6 us
    ppermute x4, starting transfers between devices, apply(): beside = lax.ppermute(copied, 'lgroup', swaps(blocks, 0))  13.9 us
    ppermute x4, starting transfers between devices, apply(): across = lax.ppermute(message, 'lgroup', swaps(blocks, 1))  12.8 us
    ppermute x4, starting transfers between devices, apply(): below = lax.ppermute(high, 'row', shifts(strips, 1))  9.14 us
    ppermute x4, waiting for transfers between devices, apply(): across = lax.ppermute(message, 'lgroup', swaps(blocks, 1))  7.67 us
    pallas_call x9, Pallas kernels, call(): pl.pallas_call(kernel, out_shape=outs, cost_estimate=cost, compiler_param...  5.5 us
  transfers between devices with their start and end apart: 18, of which 4 were waited for; matrix products, arithmetic and copies ran while one was open for 4% of the time, Pallas kernels for 1%

profile of v2, /device:TPU:262, one launch (start us, length us, event | category | flops | bytes accessed | tf_op | source)
XLA Modules:
  0.0 163.7 jit_solution(2261810405960894715)
XLA Ops:
  0.0 1.3 fusion.5
  2.6 15.6 %all-to-all-start = ((f32[8,8,128]{2,1,0:T(8,128)}), f32[8,8,128]{2,1,0:T(8,128)}, u32[]{:S(2)}, u32[]{:S(2)}) async-start(f32[8,8,128]{2,1,0:T(8,128)} %broadcast_in_dim.7), calls=%async_computation | async-start | bytes 65536 | tf_op jit(solution)/shard_map/all_to_all | solution.py:188
  19.0 2.0 %collective-permute-start.76 = (f32[2,64,64]{1,2,0:T(8,128)}, f32[2,64,64]{1,2,0:T(8,128)S(1)}, u32[]{:S(2)}, u32[]{:S(2)}) collective-permute-start(f32[2,64,64]{1,2,0:T(8,128)} %copy.19), channel_id=1, source_target_pairs={{0,128},{128,256},{256,384},{384,512},{512,640},{640,768},{768,896... | collective-permute-start | bytes 98312 | tf_op jit(solution)/shard_map/ppermute | solution.py:202
  21.1 1.0 copy-done
  22.5 3.4 %collective-permute-start.74 = (f32[2,2,64,128]{3,2,1,0:T(8,128)S(1)}, f32[2,2,64,128]{3,2,1,0:T(8,128)S(1)}, u32[]{:S(2)}, u32[]{:S(2)}) collective-permute-start(f32[2,2,64,128]{3,2,1,0:T(8,128)S(1)} %get-tuple-element.326), channel_id=1, source_target_pairs={{0,1},{1,2},{2,3},{3,4},{4,5},{5,6},{6,7},{7,8},{8,9},{9,10},{10,1... | collective-permute-start | bytes 393224 | tf_op jit(solution)/shard_map/ppermute | solution.py:218
  25.9 7.3 %collective-permute-start.75 = (f32[2,2,64,128]{3,2,1,0:T(8,128)S(1)}, f32[2,2,64,128]{3,2,1,0:T(8,128)S(1)}, u32[]{:S(2)}, u32[]{:S(2)}) collective-permute-start(f32[2,2,64,128]{3,2,1,0:T(8,128)S(1)} %get-tuple-element.327), channel_id=1, source_target_pairs={{1,0},{2,1},{3,2},{4,3},{5,4},{6,5},{7,6},{8,7},{9,8},{10,9},{11,1... | collective-permute-start | bytes 393224 | tf_op jit(solution)/shard_map/ppermute | solution.py:219
  34.1 0.7 shard_map.62
  34.9 0.8 copy-done.1
  35.7 6.8 %collective-permute-start.72 = (f32[2,8,64,128]{3,2,1,0:T(8,128)S(1)}, f32[2,8,64,128]{3,2,1,0:T(8,128)S(1)}, u32[]{:S(2)}, u32[]{:S(2)}) collective-permute-start(f32[2,8,64,128]{3,2,1,0:T(8,128)S(1)} %get-tuple-element.324), channel_id=1, source_target_pairs={{128,256},{256,128},{384,512},{512,384},{640,768},{768,640},{129,2... | collective-permute-start | bytes 1572872 | tf_op jit(solution)/shard_map/ppermute | solution.py:216
  42.5 2.5 %collective-permute-start.73 = (f32[2,8,64,128]{3,2,1,0:T(8,128)S(1)}, f32[2,8,64,128]{3,2,1,0:T(8,128)S(1)}, u32[]{:S(2)}, u32[]{:S(2)}) collective-permute-start(f32[2,8,64,128]{3,2,1,0:T(8,128)S(1)} %get-tuple-element.325), channel_id=1, source_target_pairs={{0,128},{128,0},{256,384},{384,256},{512,640},{640,512},{768,896},... | collective-permute-start | bytes 1572872 | tf_op jit(solution)/shard_map/ppermute | solution.py:217
  46.4 0.9 reduce-precision_convert_fusion.1
  48.2 0.9 slice_reduce_fusion
  54.5 7.7 %collective-permute-done.72.across_ref = f32[2,8,64,128]{3,2,1,0:T(8,128)S(1)} collective-permute-done((f32[2,8,64,128]{3,2,1,0:T(8,128)S(1)}, f32[2,8,64,128]{3,2,1,0:T(8,128)S(1)}, u32[]{:S(2)}, u32[]{:S(2)}) %collective-permute-start.72) | collective-permute-done | bytes 524320 | tf_op jit(solution)/shard_map/ppermute | solution.py:216
  62.2 1.0 copy-done.2
  64.2 98.7 %conditional.1 = (f32[2,64,8,128]{3,2,1,0:T(8,128)S(1)}) conditional(s32[]{:T(128)} %clamp.3, (f32[2,8,64,128]{3,2,1,0:T(8,128)S(1)}, bf16[192,192]{1,0:T(8,128)(2,1)S(1)}, bf16[128,192]{1,0:T(8,128)(2,1)S(1)}, f32[8,8,128]{2,1,0:T(8,128)S(1)}, f32[8,64,128]{2,1,0:T(8,128)S(1)}, ...), branch_computations={%region_4.5_spmd, %region_5.6_spmd, %region_6.7_spmd, %region_7.8_... | conditional | flops 4800000000 | bytes 33729128 | solution.py:240
  64.9 7.6 %collective-permute-start.37 = (f32[2,8,64,128]{3,2,1,0:T(8,128)S(1)}, f32[2,8,64,128]{3,2,1,0:T(8,128)S(1)}, u32[]{:S(2)}, u32[]{:S(2)}) collective-permute-start(f32[2,8,64,128]{3,2,1,0:T(8,128)S(1)} %get-tuple-element.235), channel_id=1, source_target_pairs={{0,128},{128,0},{256,384},{384,256},{512,640},{640,512},{768,896},... | collective-permute-start | bytes 1572872 | tf_op jit(solution)/shard_map/cond/branch_3_fun/ppermute | solution.py:217
  72.5 2.1 %collective-permute-start.36 = (f32[2,8,48,128]{3,2,1,0:T(8,128)S(1)}, f32[2,8,48,128]{3,2,1,0:T(8,128)S(1)}, u32[]{:S(2)}, u32[]{:S(2)}) collective-permute-start(f32[2,8,48,128]{3,2,1,0:T(8,128)S(1)} %get-tuple-element.234), channel_id=1, source_target_pairs={{128,256},{256,128},{384,512},{512,384},{640,768},{768,640},{129,2... | collective-permute-start | bytes 1179656 | tf_op jit(solution)/shard_map/cond/branch_3_fun/ppermute | solution.py:216
  74.6 1.9 %collective-permute-start.38 = (f32[2,2,64,128]{3,2,1,0:T(8,128)S(1)}, f32[2,2,64,128]{3,2,1,0:T(8,128)S(1)}, u32[]{:S(2)}, u32[]{:S(2)}) collective-permute-start(f32[2,2,64,128]{3,2,1,0:T(8,128)S(1)} %get-tuple-element.236), channel_id=1, source_target_pairs={{0,1},{1,2},{2,3},{3,4},{4,5},{5,6},{6,7},{7,8},{8,9},{9,10},{10,1... | collective-permute-start | bytes 393224 | tf_op jit(solution)/shard_map/cond/branch_3_fun/ppermute | solution.py:218
  76.5 8.7 %collective-permute-start.39 = (f32[2,2,64,128]{3,2,1,0:T(8,128)S(1)}, f32[2,2,64,128]{3,2,1,0:T(8,128)S(1)}, u32[]{:S(2)}, u32[]{:S(2)}) collective-permute-start(f32[2,2,64,128]{3,2,1,0:T(8,128)S(1)} %get-tuple-element.237), channel_id=1, source_target_pairs={{1,0},{2,1},{3,2},{4,3},{5,4},{6,5},{7,6},{8,7},{9,8},{10,9},{11,1... | collective-permute-start | bytes 393224 | tf_op jit(solution)/shard_map/cond/branch_3_fun/ppermute | solution.py:219
  85.2 11.8 %collective-permute-done.38.below_ref = f32[2,2,64,128]{3,2,1,0:T(8,128)S(1)} collective-permute-done((f32[2,2,64,128]{3,2,1,0:T(8,128)S(1)}, f32[2,2,64,128]{3,2,1,0:T(8,128)S(1)}, u32[]{:S(2)}, u32[]{:S(2)}) %collective-permute-start.38) | collective-permute-done | bytes 131104 | tf_op jit(solution)/shard_map/cond/branch_3_fun/ppermute | solution.py:218
  98.3 1.9 %collective-permute-start.41 = (f32[2,8,64,128]{3,2,1,0:T(8,128)S(1)}, f32[2,8,64,128]{3,2,1,0:T(8,128)S(1)}, u32[]{:S(2)}, u32[]{:S(2)}) collective-permute-start(f32[2,8,64,128]{3,2,1,0:T(8,128)S(1)} %get-tuple-element.245), channel_id=1, source_target_pairs={{0,128},{128,0},{256,384},{384,256},{512,640},{640,512},{768,896},... | collective-permute-start | bytes 1572872 | tf_op jit(solution)/shard_map/cond/branch_3_fun/ppermute | solution.py:217
  100.2 1.9 %collective-permute-start.40 = (f32[2,8,48,128]{3,2,1,0:T(8,128)S(1)}, f32[2,8,48,128]{3,2,1,0:T(8,128)S(1)}, u32[]{:S(2)}, u32[]{:S(2)}) collective-permute-start(f32[2,8,48,128]{3,2,1,0:T(8,128)S(1)} %get-tuple-element.244), channel_id=1, source_target_pairs={{128,256},{256,128},{384,512},{512,384},{640,768},{768,640},{129,2... | collective-permute-start | bytes 1179656 | tf_op jit(solution)/shard_map/cond/branch_3_fun/ppermute | solution.py:216
  102.2 1.9 %collective-permute-start.42 = (f32[2,2,64,128]{3,2,1,0:T(8,128)S(1)}, f32[2,2,64,128]{3,2,1,0:T(8,128)S(1)}, u32[]{:S(2)}, u32[]{:S(2)}) collective-permute-start(f32[2,2,64,128]{3,2,1,0:T(8,128)S(1)} %get-tuple-element.246), channel_id=1, source_target_pairs={{0,1},{1,2},{2,3},{3,4},{4,5},{5,6},{6,7},{7,8},{8,9},{9,10},{10,1... | collective-permute-start | bytes 393224 | tf_op jit(solution)/shard_map/cond/branch_3_fun/ppermute | solution.py:218
  104.1 8.7 %collective-permute-start.43 = (f32[2,2,64,128]{3,2,1,0:T(8,128)S(1)}, f32[2,2,64,128]{3,2,1,0:T(8,128)S(1)}, u32[]{:S(2)}, u32[]{:S(2)}) collective-permute-start(f32[2,2,64,128]{3,2,1,0:T(8,128)S(1)} %get-tuple-element.247), channel_id=1, source_target_pairs={{1,0},{2,1},{3,2},{4,3},{5,4},{6,5},{7,6},{8,7},{9,8},{10,9},{11,1... | collective-permute-start | bytes 393224 | tf_op jit(solution)/shard_map/cond/branch_3_fun/ppermute | solution.py:219
  112.8 15.5 %collective-permute-done.42.below_ref = f32[2,2,64,128]{3,2,1,0:T(8,128)S(1)} collective-permute-done((f32[2,2,64,128]{3,2,1,0:T(8,128)S(1)}, f32[2,2,64,128]{3,2,1,0:T(8,128)S(1)}, u32[]{:S(2)}, u32[]{:S(2)}) %collective-permute-start.42) | collective-permute-done | bytes 131104 | tf_op jit(solution)/shard_map/cond/branch_3_fun/ppermute | solution.py:218
  129.6 1.9 %collective-permute-start.45 = (f32[2,8,64,128]{3,2,1,0:T(8,128)S(1)}, f32[2,8,64,128]{3,2,1,0:T(8,128)S(1)}, u32[]{:S(2)}, u32[]{:S(2)}) collective-permute-start(f32[2,8,64,128]{3,2,1,0:T(8,128)S(1)} %get-tuple-element.252), channel_id=1, source_target_pairs={{0,128},{128,0},{256,384},{384,256},{512,640},{640,512},{768,896},... | collective-permute-start | bytes 1572872 | tf_op jit(solution)/shard_map/cond/branch_3_fun/ppermute | solution.py:217
  131.6 1.9 %collective-permute-start.44 = (f32[2,8,48,128]{3,2,1,0:T(8,128)S(1)}, f32[2,8,48,128]{3,2,1,0:T(8,128)S(1)}, u32[]{:S(2)}, u32[]{:S(2)}) collective-permute-start(f32[2,8,48,128]{3,2,1,0:T(8,128)S(1)} %get-tuple-element.251), channel_id=1, source_target_pairs={{128,256},{256,128},{384,512},{512,384},{640,768},{768,640},{129,2... | collective-permute-start | bytes 1179656 | tf_op jit(solution)/shard_map/cond/branch_3_fun/ppermute | solution.py:216
  133.5 1.9 %collective-permute-start.46 = (f32[2,2,64,128]{3,2,1,0:T(8,128)S(1)}, f32[2,2,64,128]{3,2,1,0:T(8,128)S(1)}, u32[]{:S(2)}, u32[]{:S(2)}) collective-permute-start(f32[2,2,64,128]{3,2,1,0:T(8,128)S(1)} %get-tuple-element.253), channel_id=1, source_target_pairs={{0,1},{1,2},{2,3},{3,4},{4,5},{5,6},{6,7},{7,8},{8,9},{9,10},{10,1... | collective-permute-start | bytes 393224 | tf_op jit(solution)/shard_map/cond/branch_3_fun/ppermute | solution.py:218
  135.4 8.7 %collective-permute-start.47 = (f32[2,2,64,128]{3,2,1,0:T(8,128)S(1)}, f32[2,2,64,128]{3,2,1,0:T(8,128)S(1)}, u32[]{:S(2)}, u32[]{:S(2)}) collective-permute-start(f32[2,2,64,128]{3,2,1,0:T(8,128)S(1)} %get-tuple-element.254), channel_id=1, source_target_pairs={{1,0},{2,1},{3,2},{4,3},{5,4},{6,5},{7,6},{8,7},{9,8},{10,9},{11,1... | collective-permute-start | bytes 393224 | tf_op jit(solution)/shard_map/cond/branch_3_fun/ppermute | solution.py:219
  144.2 17.7 %collective-permute-done.46.below_ref = f32[2,2,64,128]{3,2,1,0:T(8,128)S(1)} collective-permute-done((f32[2,2,64,128]{3,2,1,0:T(8,128)S(1)}, f32[2,2,64,128]{3,2,1,0:T(8,128)S(1)}, u32[]{:S(2)}, u32[]{:S(2)}) %collective-permute-start.46) | collective-permute-done | bytes 131104 | tf_op jit(solution)/shard_map/cond/branch_3_fun/ppermute | solution.py:218
  161.9 0.7 branch_3_fun.11
  162.9 0.8 copy-done.13
  (89 shorter events, 11.9 us)
Async XLA Ops:
  0.0 18.3 %copy-start.3 = (f32[1,2,64,64]{3,2,1,0:T(8,128)S(1)}, f32[1,2,64,64]{3,2,1,0:T(8,128)}, u32[]{:S(2)}) copy-start(f32[1,2,64,64]{3,2,1,0:T(8,128)} %param.14) | copy-start | bytes 98308
  2.6 45.5 %all-to-all-start = ((f32[8,8,128]{2,1,0:T(8,128)}), f32[8,8,128]{2,1,0:T(8,128)}, u32[]{:S(2)}, u32[]{:S(2)}) async-start(f32[8,8,128]{2,1,0:T(8,128)} %broadcast_in_dim.7), calls=%async_computation | async-start | bytes 65536 | tf_op jit(solution)/shard_map/all_to_all | solution.py:188
  18.3 2.8 %copy-start.12 = (s32[1,2,64]{2,1,0:T(2,128)S(1)}, s32[1,2,64]{2,1,0:T(2,128)}, u32[]{:S(2)}) copy-start(s32[1,2,64]{2,1,0:T(2,128)} %param.12) | copy-start | bytes 1540
  19.0 26.7 %collective-permute-start.76 = (f32[2,64,64]{1,2,0:T(8,128)}, f32[2,64,64]{1,2,0:T(8,128)S(1)}, u32[]{:S(2)}, u32[]{:S(2)}) collective-permute-start(f32[2,64,64]{1,2,0:T(8,128)} %copy.19), channel_id=1, source_target_pairs={{0,128},{128,256},{256,384},{384,512},{512,640},{640,768},{768,896... | collective-permute-start | bytes 98312 | tf_op jit(solution)/shard_map/ppermute | solution.py:202
  21.1 1.0 copy-start
  22.2 11.1 %copy-start.4 = (f32[1,3,64,64]{3,2,1,0:T(8,128)S(1)}, f32[1,3,64,64]{3,2,1,0:T(8,128)}, u32[]{:S(2)}) copy-start(f32[1,3,64,64]{3,2,1,0:T(8,128)} %param.13) | copy-start | bytes 147460
  22.5 32.0 %collective-permute-start.74 = (f32[2,2,64,128]{3,2,1,0:T(8,128)S(1)}, f32[2,2,64,128]{3,2,1,0:T(8,128)S(1)}, u32[]{:S(2)}, u32[]{:S(2)}) collective-permute-start(f32[2,2,64,128]{3,2,1,0:T(8,128)S(1)} %get-tuple-element.326), channel_id=1, source_target_pairs={{0,1},{1,2},{2,3},{3,4},{4,5},{5,6},{6,7},{7,8},{8,9},{9,10},{10,1... | collective-permute-start | bytes 393224 | tf_op jit(solution)/shard_map/ppermute | solution.py:218
  25.9 28.6 %collective-permute-start.75 = (f32[2,2,64,128]{3,2,1,0:T(8,128)S(1)}, f32[2,2,64,128]{3,2,1,0:T(8,128)S(1)}, u32[]{:S(2)}, u32[]{:S(2)}) collective-permute-start(f32[2,2,64,128]{3,2,1,0:T(8,128)S(1)} %get-tuple-element.327), channel_id=1, source_target_pairs={{1,0},{2,1},{3,2},{4,3},{5,4},{6,5},{7,6},{8,7},{9,8},{10,9},{11,1... | collective-permute-start | bytes 393224 | tf_op jit(solution)/shard_map/ppermute | solution.py:219
  34.0 0.9 copy-start.5
  34.1 11.0 %copy-start.7 = (f32[8,1,128]{2,1,0:T(1,128)}, f32[8,1,128]{2,1,0:T(1,128)S(1)}, u32[]{:S(2)}) copy-start(f32[8,1,128]{2,1,0:T(1,128)S(1)} %stack_broadcast_in_dim.11) | copy-start | bytes 12292
  34.9 0.8 copy-start.1
  35.7 26.5 %collective-permute-start.72 = (f32[2,8,64,128]{3,2,1,0:T(8,128)S(1)}, f32[2,8,64,128]{3,2,1,0:T(8,128)S(1)}, u32[]{:S(2)}, u32[]{:S(2)}) collective-permute-start(f32[2,8,64,128]{3,2,1,0:T(8,128)S(1)} %get-tuple-element.324), channel_id=1, source_target_pairs={{128,256},{256,128},{384,512},{512,384},{640,768},{768,640},{129,2... | collective-permute-start | bytes 1572872 | tf_op jit(solution)/shard_map/ppermute | solution.py:216
  42.5 19.6 %collective-permute-start.73 = (f32[2,8,64,128]{3,2,1,0:T(8,128)S(1)}, f32[2,8,64,128]{3,2,1,0:T(8,128)S(1)}, u32[]{:S(2)}, u32[]{:S(2)}) collective-permute-start(f32[2,8,64,128]{3,2,1,0:T(8,128)S(1)} %get-tuple-element.325), channel_id=1, source_target_pairs={{0,128},{128,0},{256,384},{384,256},{512,640},{640,512},{768,896},... | collective-permute-start | bytes 1572872 | tf_op jit(solution)/shard_map/ppermute | solution.py:217
  51.9 0.7 copy-start.14
  53.7 0.7 copy-start.8
  53.8 0.7 copy-start.10
  62.2 1.0 copy-start.2
  63.2 0.9 copy-start.6
  63.2 1.0 copy-start.11
  64.9 32.1 %collective-permute-start.37 = (f32[2,8,64,128]{3,2,1,0:T(8,128)S(1)}, f32[2,8,64,128]{3,2,1,0:T(8,128)S(1)}, u32[]{:S(2)}, u32[]{:S(2)}) collective-permute-start(f32[2,8,64,128]{3,2,1,0:T(8,128)S(1)} %get-tuple-element.235), channel_id=1, source_target_pairs={{0,128},{128,0},{256,384},{384,256},{512,640},{640,512},{768,896},... | collective-permute-start | bytes 1572872 | tf_op jit(solution)/shard_map/cond/branch_3_fun/ppermute | solution.py:217
  72.5 24.6 %collective-permute-start.36 = (f32[2,8,48,128]{3,2,1,0:T(8,128)S(1)}, f32[2,8,48,128]{3,2,1,0:T(8,128)S(1)}, u32[]{:S(2)}, u32[]{:S(2)}) collective-permute-start(f32[2,8,48,128]{3,2,1,0:T(8,128)S(1)} %get-tuple-element.234), channel_id=1, source_target_pairs={{128,256},{256,128},{384,512},{512,384},{640,768},{768,640},{129,2... | collective-permute-start | bytes 1179656 | tf_op jit(solution)/shard_map/cond/branch_3_fun/ppermute | solution.py:216
  74.6 22.5 %collective-permute-start.38 = (f32[2,2,64,128]{3,2,1,0:T(8,128)S(1)}, f32[2,2,64,128]{3,2,1,0:T(8,128)S(1)}, u32[]{:S(2)}, u32[]{:S(2)}) collective-permute-start(f32[2,2,64,128]{3,2,1,0:T(8,128)S(1)} %get-tuple-element.236), channel_id=1, source_target_pairs={{0,1},{1,2},{2,3},{3,4},{4,5},{5,6},{6,7},{7,8},{8,9},{9,10},{10,1... | collective-permute-start | bytes 393224 | tf_op jit(solution)/shard_map/cond/branch_3_fun/ppermute | solution.py:218
  76.5 20.5 %collective-permute-start.39 = (f32[2,2,64,128]{3,2,1,0:T(8,128)S(1)}, f32[2,2,64,128]{3,2,1,0:T(8,128)S(1)}, u32[]{:S(2)}, u32[]{:S(2)}) collective-permute-start(f32[2,2,64,128]{3,2,1,0:T(8,128)S(1)} %get-tuple-element.237), channel_id=1, source_target_pairs={{1,0},{2,1},{3,2},{4,3},{5,4},{6,5},{7,6},{8,7},{9,8},{10,9},{11,1... | collective-permute-start | bytes 393224 | tf_op jit(solution)/shard_map/cond/branch_3_fun/ppermute | solution.py:219
  98.3 30.1 %collective-permute-start.41 = (f32[2,8,64,128]{3,2,1,0:T(8,128)S(1)}, f32[2,8,64,128]{3,2,1,0:T(8,128)S(1)}, u32[]{:S(2)}, u32[]{:S(2)}) collective-permute-start(f32[2,8,64,128]{3,2,1,0:T(8,128)S(1)} %get-tuple-element.245), channel_id=1, source_target_pairs={{0,128},{128,0},{256,384},{384,256},{512,640},{640,512},{768,896},... | collective-permute-start | bytes 1572872 | tf_op jit(solution)/shard_map/cond/branch_3_fun/ppermute | solution.py:217
  100.2 28.1 %collective-permute-start.40 = (f32[2,8,48,128]{3,2,1,0:T(8,128)S(1)}, f32[2,8,48,128]{3,2,1,0:T(8,128)S(1)}, u32[]{:S(2)}, u32[]{:S(2)}) collective-permute-start(f32[2,8,48,128]{3,2,1,0:T(8,128)S(1)} %get-tuple-element.244), channel_id=1, source_target_pairs={{128,256},{256,128},{384,512},{512,384},{640,768},{768,640},{129,2... | collective-permute-start | bytes 1179656 | tf_op jit(solution)/shard_map/cond/branch_3_fun/ppermute | solution.py:216
  102.2 26.2 %collective-permute-start.42 = (f32[2,2,64,128]{3,2,1,0:T(8,128)S(1)}, f32[2,2,64,128]{3,2,1,0:T(8,128)S(1)}, u32[]{:S(2)}, u32[]{:S(2)}) collective-permute-start(f32[2,2,64,128]{3,2,1,0:T(8,128)S(1)} %get-tuple-element.246), channel_id=1, source_target_pairs={{0,1},{1,2},{2,3},{3,4},{4,5},{5,6},{6,7},{7,8},{8,9},{9,10},{10,1... | collective-permute-start | bytes 393224 | tf_op jit(solution)/shard_map/cond/branch_3_fun/ppermute | solution.py:218
  104.1 24.3 %collective-permute-start.43 = (f32[2,2,64,128]{3,2,1,0:T(8,128)S(1)}, f32[2,2,64,128]{3,2,1,0:T(8,128)S(1)}, u32[]{:S(2)}, u32[]{:S(2)}) collective-permute-start(f32[2,2,64,128]{3,2,1,0:T(8,128)S(1)} %get-tuple-element.247), channel_id=1, source_target_pairs={{1,0},{2,1},{3,2},{4,3},{5,4},{6,5},{7,6},{8,7},{9,8},{10,9},{11,1... | collective-permute-start | bytes 393224 | tf_op jit(solution)/shard_map/cond/branch_3_fun/ppermute | solution.py:219
  129.6 32.2 %collective-permute-start.45 = (f32[2,8,64,128]{3,2,1,0:T(8,128)S(1)}, f32[2,8,64,128]{3,2,1,0:T(8,128)S(1)}, u32[]{:S(2)}, u32[]{:S(2)}) collective-permute-start(f32[2,8,64,128]{3,2,1,0:T(8,128)S(1)} %get-tuple-element.252), channel_id=1, source_target_pairs={{0,128},{128,0},{256,384},{384,256},{512,640},{640,512},{768,896},... | collective-permute-start | bytes 1572872 | tf_op jit(solution)/shard_map/cond/branch_3_fun/ppermute | solution.py:217
  131.6 30.3 %collective-permute-start.44 = (f32[2,8,48,128]{3,2,1,0:T(8,128)S(1)}, f32[2,8,48,128]{3,2,1,0:T(8,128)S(1)}, u32[]{:S(2)}, u32[]{:S(2)}) collective-permute-start(f32[2,8,48,128]{3,2,1,0:T(8,128)S(1)} %get-tuple-element.251), channel_id=1, source_target_pairs={{128,256},{256,128},{384,512},{512,384},{640,768},{768,640},{129,2... | collective-permute-start | bytes 1179656 | tf_op jit(solution)/shard_map/cond/branch_3_fun/ppermute | solution.py:216
  133.5 28.3 %collective-permute-start.46 = (f32[2,2,64,128]{3,2,1,0:T(8,128)S(1)}, f32[2,2,64,128]{3,2,1,0:T(8,128)S(1)}, u32[]{:S(2)}, u32[]{:S(2)}) collective-permute-start(f32[2,2,64,128]{3,2,1,0:T(8,128)S(1)} %get-tuple-element.253), channel_id=1, source_target_pairs={{0,1},{1,2},{2,3},{3,4},{4,5},{5,6},{6,7},{7,8},{8,9},{9,10},{10,1... | collective-permute-start | bytes 393224 | tf_op jit(solution)/shard_map/cond/branch_3_fun/ppermute | solution.py:218
  135.4 26.4 %collective-permute-start.47 = (f32[2,2,64,128]{3,2,1,0:T(8,128)S(1)}, f32[2,2,64,128]{3,2,1,0:T(8,128)S(1)}, u32[]{:S(2)}, u32[]{:S(2)}) collective-permute-start(f32[2,2,64,128]{3,2,1,0:T(8,128)S(1)} %get-tuple-element.254), channel_id=1, source_target_pairs={{1,0},{2,1},{3,2},{4,3},{5,4},{6,5},{7,6},{8,7},{9,8},{10,9},{11,1... | collective-permute-start | bytes 393224 | tf_op jit(solution)/shard_map/cond/branch_3_fun/ppermute | solution.py:219
  162.9 0.8 copy-start.13
  (1 other events, 0.6 us)
